TPU v7x, 256 devices: a whole 4x4x8 slice. The times are simulated.
256 devices in a mesh: chan: 128 (over x, z, y), radial: 2 (over core).
Axes of the slice: x: 4, y: 4, z: 8, core: 2. Of those that a mesh axis runs over, the one named last changes fastest.
Arguments:
- wave: bfloat16 [512, 2, 6, 256, 384], P('chan', None, None, 'radial'), may hold values from -6 to 6
- l_values: int32 [512, 3], P('chan'), may hold values from 0 to 3
- couple_source: int32 [512, 8], replicated, may hold values from 0 to 511, as said below
- couple_pair: int32 [512, 8], P('chan'), may hold values from 0 to 2
- couple_order: int32 [512, 8], P('chan'), may hold values from 0 to 3
- couple_weight: float32 [512, 8], P('chan'), may hold values from -4 to 4
- channel_slot: int32 [512], replicated, may hold values from 0 to 511, as said below
Outputs:
- diag_step: bfloat16 [512, 2, 4, 256, 384], P('chan', None, None, 'radial')
- coupling_rate: bfloat16 [512, 2, 4, 256, 384], P('chan', None, None, 'radial')
Inputs may be any that keep to these rules, and one draw needn't show every extreme that they name: `couple_source`: with slot = channel_slot of an entry's source and the entry's own slot, slot // 4 of the two differ by at most 2; the entries of the 4 channels in the slots of one device name at most 2 distinct source channels whose slots lie on any one other device, and exactly 2 for some device and every offset up to 2. Each channel has 8 entries. `channel_slot`: A permutation: the slot of each channel.
All inputs are finite; a program needn't handle non-finite values.
Results may differ from a plain program's by a relative error of at most 0.001.
Values may be sent and summed in bfloat16 or wider, within the bound.
No kernel may reach another device: no remote copies, remote signals or barrier semaphores. Data moves between devices by JAX's collectives and lax.ppermute only.
A program may use at most 192 MiB of HBM per device.

v0:
```python
import functools

import jax
import jax.numpy as jnp
from jax import lax
from jax.experimental import pallas as pl
from jax.experimental.pallas import tpu as pltpu
from jax.sharding import PartitionSpec as P

WSTART = 16
grid_step = 0.25
charge = 3.0
time_step = 0.02

HELD = 4
PARTS = 8
PLANES = 4
ORDERS = 4
LISTED = 3
ENTRIES = HELD * PARTS
GROUPS = 7

PAIR_LOW = 1233667140
PAIR_HIGH = 1234062796


def two_of(mask):
    word = jnp.where(mask >= 8, PAIR_HIGH, PAIR_LOW)
    code = lax.shift_right_logical(word, 4 * (mask & 7)) & 15
    return code & 3, code >> 2


def needed(source_ref, slot_ref, device, offset, devices):
    reader = device + offset
    inside = (reader >= 0) & (reader < devices)
    row = jnp.clip(reader, 0, devices - 1) * HELD
    mask = jnp.int32(0)
    for i in range(HELD):
        for e in range(PARTS):
            slot = slot_ref[source_ref[e, row + i]]
            mask = mask | jnp.where(slot // HELD == device, jnp.int32(1) << (slot % HELD), 0)
    return two_of(jnp.where(inside, mask, 0))


def listed(first, second, pair):
    l1 = jnp.where(second != first, second, jnp.where(pair[0] != first, pair[0], pair[1]))
    l2 = jnp.where((pair[0] == first) | (pair[0] == l1), pair[1], pair[0])
    return first, l1, l2


def plan(source_ref, slot_ref, device, devices):
    near_up = needed(source_ref, slot_ref, device, 1, devices)
    near_down = needed(source_ref, slot_ref, device, -1, devices)
    far_up = needed(source_ref, slot_ref, device, 2, devices)
    far_down = needed(source_ref, slot_ref, device, -2, devices)

    def outside(value, pair):
        return (value != pair[0]) & (value != pair[1])

    best = None
    for a in (1, 0):
        for c in (1, 0):
            a_up, a_down = far_up[a], far_up[1 - a]
            c_up, c_down = far_down[c], far_down[1 - c]
            bad = (a_up != c_up) & outside(a_up, near_up) & outside(c_up, near_up)
            bad = bad | ((a_down != c_down) & outside(a_down, near_down) & outside(c_down, near_down))
            here = (a_up, a_down, c_up, c_down)
            if best is None:
                best = here
            else:
                best = tuple(jnp.where(bad, old, new) for old, new in zip(best, here))
    a_up, a_down, c_up, c_down = best
    up = listed(a_up, c_up, near_up)
    down = listed(c_down, a_down, near_down)
    return up, down, best


def run(copies):
    for copy in copies:
        copy.start()
    for copy in copies:
        copy.wait()


def gather(wave_ref, picks_ref, out_refs, sem, planes):
    copies = []
    for plane, (up_ref, down_ref) in zip(planes, out_refs):
        for i in range(LISTED):
            for base, ref in ((0, up_ref), (LISTED, down_ref)):
                copies.append(
                    pltpu.make_async_copy(
                        wave_ref.at[picks_ref[base + i], :, 1 + plane],
                        ref.at[i],
                        sem.at[len(copies)],
                    )
                )
    run(copies)


def first_kernel(
    devices, planes, me_ref, sources, slots, wave_ref, picks_ref, up_ref, down_ref, source_ref, slot_ref, sem
):
    run([
        pltpu.make_async_copy(sources, source_ref, sem.at[0]),
        pltpu.make_async_copy(slots, slot_ref, sem.at[1]),
    ])
    up, down, _ = plan(source_ref, slot_ref, me_ref[0], devices)
    for i in range(LISTED):
        picks_ref[i] = up[i]
        picks_ref[LISTED + i] = down[i]
    gather(wave_ref, picks_ref, [(up_ref, down_ref)], sem, planes)


def rest_kernel(planes, picks_ref, wave_ref, *refs):
    outs, sem = refs[:-1], refs[-1]
    gather(wave_ref, picks_ref, list(zip(outs[0::2], outs[1::2])), sem, planes)


def item_kernel(
    devices, me_ref, sources, slots, pair_ref, order_ref, count_ref, item_ref, pass_ref, source_ref, slot_ref, sem
):
    run([
        pltpu.make_async_copy(sources, source_ref, sem.at[0]),
        pltpu.make_async_copy(slots, slot_ref, sem.at[1]),
    ])
    me = me_ref[0]
    before = lax.rem(me + devices - 1, devices)
    after = lax.rem(me + 1, devices)
    up_before, _, far_before = plan(source_ref, slot_ref, before, devices)
    _, down_after, far_after = plan(source_ref, slot_ref, after, devices)
    pass_ref[0] = jnp.where(far_before[2] == far_before[0], 0, 1)
    pass_ref[1] = jnp.where(far_after[1] == far_after[3], 0, 1)
    _, _, far_two_before = plan(source_ref, slot_ref, lax.rem(me + devices - 2, devices), devices)
    _, _, far_two_after = plan(source_ref, slot_ref, lax.rem(me + 2, devices), devices)

    def among(value, three):
        return jnp.where(value == three[0], 0, jnp.where(value == three[1], 1, 2))

    for g in range(GROUPS):
        count_ref[g] = jnp.int32(0)
    for s in range(HELD):
        for e in range(PARTS):
            slot = slot_ref[source_ref[e, me * HELD + s]]
            local, offset = slot % HELD, slot // HELD - me
            group = jnp.where(offset == -1, 1, jnp.where(offset == 1, 2, 0))
            group = jnp.where(offset == -2, jnp.where(local == far_two_before[0], 3, 4), group)
            group = jnp.where(offset == 2, jnp.where(local == far_two_after[3], 5, 6), group)
            place = jnp.where(group == 0, local, 0)
            place = jnp.where(group == 1, among(local, up_before), place)
            place = jnp.where(group == 2, among(local, down_after), place)
            field = pair_ref[s, e] * ORDERS + order_ref[s, e]
            number = count_ref[group]
            item_ref[group, number] = (s * PARTS + e) + ENTRIES * (place + HELD * field)
            count_ref[group] = number + 1


def pass_kernel(pass_ref, up_ref, down_ref, up_one, down_one, down_three, up_three):
    up_one[...] = up_ref[0]
    down_one[...] = down_ref[0]
    down_three[...] = up_ref[pass_ref[0]]
    up_three[...] = down_ref[pass_ref[1]]


def radius(shape, dim, start):
    return (start + lax.broadcasted_iota(jnp.int32, shape, dim) + 1).astype(jnp.float32) * grid_step


def field_kernel(row_ref, *out_refs):
    shape = out_refs[0].shape[1:]
    step = 16

    def tile(i, carry):
        at = pl.ds(pl.multiple_of(i * step, step), step)
        part = (step, shape[1])
        r_one = radius(part, 0, row_ref[0] + i * step)
        r_two = radius(part, 1, 0)

        def write(refs, pair, left, right):
            greater = jnp.maximum(left, right)
            value = 1.0 / greater
            ratio = jnp.minimum(left, right) / greater
            for order in range(ORDERS):
                for ref in refs:
                    ref[pair * ORDERS + order, at] = jnp.broadcast_to(value, part)
                value = value * ratio

        write(out_refs, 0, r_one, r_two)
        for p, ref in enumerate(out_refs):
            r_three = (WSTART + p + 1) * grid_step
            write([ref], 1, r_one, r_three)
            write([ref], 2, r_two, r_three)
        return carry

    lax.fori_loop(0, shape[0] // step, tile, 0)


def diagonal_kernel(row_ref, l_ref, wave_ref, edge_ref, out_ref):
    s, c = pl.program_id(0), pl.program_id(1)
    rows, columns = wave_ref.shape[3:]
    shape = (rows, columns)
    r_one = radius((rows, 1), 0, row_ref[0])
    r_two = radius((1, columns), 1, 0)

    def centrifugal(electron):
        number = l_ref[s, electron].astype(jnp.float32)
        return number * (number + 1.0)

    first = centrifugal(0) / (2.0 * r_one * r_one) - charge / r_one
    second = centrifugal(1) / (2.0 * r_two * r_two) - charge / r_two
    sign = jnp.where(c == 1, time_step, -time_step)
    lower_half = row_ref[0] == 0
    row = lax.broadcasted_iota(jnp.int32, shape, 0)
    column = lax.broadcasted_iota(jnp.int32, shape, 1)
    for p in range(PLANES):
        r_three = (WSTART + p + 1) * grid_step
        third = centrifugal(2) / (2.0 * r_three * r_three) - charge / r_three
        centre = wave_ref[0, 0, p + 1].astype(jnp.float32)
        edge = edge_ref[0, 0, p : p + 1].astype(jnp.float32)
        above = jnp.where(lower_half, 0.0, edge)
        below = jnp.where(lower_half, edge, 0.0)
        total = wave_ref[0, 0, p].astype(jnp.float32) + wave_ref[0, 0, p + 2].astype(jnp.float32)
        total = total + jnp.where(row == 0, above, pltpu.roll(centre, 1, 0))
        total = total + jnp.where(row == rows - 1, below, pltpu.roll(centre, rows - 1, 0))
        total = total + jnp.where(column == 0, 0.0, pltpu.roll(centre, 1, 1))
        total = total + jnp.where(column == columns - 1, 0.0, pltpu.roll(centre, columns - 1, 1))
        potential = first + (second + (third + 3.0 / (grid_step * grid_step)))
        energy = potential * centre - (0.5 / (grid_step * grid_step)) * total
        out_ref[0, 0, p] = (sign * energy).astype(out_ref.dtype)


def add_items(group, count_ref, item_ref, weight_ref, field_ref, source_ref, total):
    rows = total.shape[2]
    step = 16

    def one(n, carry):
        code = item_ref[group, n]
        entry, rest = code % ENTRIES, code // ENTRIES
        s, e = entry // PARTS, entry % PARTS
        place, field = rest % HELD, rest // HELD
        weight = weight_ref[s, e]
        for i in range(rows // step):
            at = pl.ds(i * step, step)
            factor = weight * field_ref[field, at]
            for c in range(2):
                total[s, c, at] += factor * source_ref[place, c, at].astype(jnp.float32)
        return carry

    lax.fori_loop(0, count_ref[group], one, 0)


def near_kernel(
    plane, count_ref, item_ref, weight_ref, wave_ref, up_ref, down_ref, field_ref, total, own, sem
):
    copy = pltpu.make_async_copy(wave_ref.at[:, :, 1 + plane], own, sem)
    copy.start()
    total[...] = jnp.zeros_like(total)
    copy.wait()
    for group, ref in ((0, own), (1, up_ref), (2, down_ref)):
        add_items(group, count_ref, item_ref, weight_ref, field_ref, ref, total)


def far_kernel(plane, count_ref, item_ref, weight_ref, near, *refs):
    far_refs, field_ref = refs[:4], refs[4]
    out_ref, total, staged, sem = refs[-4:]
    total[...] = near[...]
    for i, ref in enumerate(far_refs):
        add_items(3 + i, count_ref, item_ref, weight_ref, field_ref, ref, total)
    copies = []
    for s in range(HELD):
        staged[s, 0] = total[s, 1].astype(staged.dtype)
        staged[s, 1] = (-total[s, 0]).astype(staged.dtype)
        copies.append(pltpu.make_async_copy(staged.at[s], out_ref.at[s, :, plane], sem.at[s]))
        copies[-1].start()
    for copy in copies:
        copy.wait()


ANY = pl.BlockSpec(memory_space=pl.ANY)
HBM = pl.BlockSpec(memory_space=pltpu.HBM)
VMEM = pl.BlockSpec(memory_space=pltpu.VMEM)
SMEM = pl.BlockSpec(memory_space=pltpu.SMEM)


def params(mib):
    return pltpu.CompilerParams(vmem_limit_bytes=mib << 20)


def cost(micros):
    return pl.CostEstimate(flops=0, bytes_accessed=micros * 3_000_000, transcendentals=0)


def behind(value, *others):
    return lax.optimization_barrier((value, others))[0]


def shards(wave, l_values, couple_source, couple_pair, couple_order, couple_weight, channel_slot):
    devices = lax.axis_size("chan")
    rows, columns = wave.shape[3:]
    me = lax.axis_index("chan").astype(jnp.int32).reshape(1)
    core = lax.axis_index("radial").astype(jnp.int32)
    row_start = (core * rows).reshape(1)
    bf16 = wave.dtype
    message = jax.ShapeDtypeStruct((LISTED, 2, rows, columns), bf16)
    one = jax.ShapeDtypeStruct((2, rows, columns), bf16)
    total = jax.ShapeDtypeStruct((HELD, 2, rows, columns), jnp.float32)
    sources = couple_source.T
    index_scratch = [pltpu.SMEM(sources.shape, jnp.int32), pltpu.SMEM(channel_slot.shape, jnp.int32)]

    def dma(number):
        return pltpu.SemaphoreType.DMA((number,))

    def shift(array, by):
        return lax.ppermute(array, "chan", [(i, (i + by) % devices) for i in range(devices)])

    picks, up0, down0 = pl.pallas_call(
        functools.partial(first_kernel, devices, [0]),
        out_shape=(jax.ShapeDtypeStruct((2 * LISTED,), jnp.int32), message, message),
        in_specs=[SMEM, HBM, HBM, HBM],
        out_specs=(SMEM, VMEM, VMEM),
        scratch_shapes=[*index_scratch, dma(2 * LISTED)],
        compiler_params=params(8),
        cost_estimate=cost(3),
        name="first_kernel",
    )(me, sources, channel_slot, wave)
    later = list(range(1, PLANES))
    rest = pl.pallas_call(
        functools.partial(rest_kernel, later),
        out_shape=[message] * (2 * len(later)),
        in_specs=[SMEM, HBM],
        out_specs=[VMEM] * (2 * len(later)),
        scratch_shapes=[dma(2 * LISTED * len(later))],
        compiler_params=params(8),
        cost_estimate=cost(2),
        name="rest_kernel",
    )(picks, wave)
    ups = [shift(v, 1) for v in [up0] + list(rest[0::2])]
    downs = [shift(v, -1) for v in [down0] + list(rest[1::2])]

    wave_late, me_late, start_late = behind((wave, me, row_start), *rest)
    edge = jnp.where(core == 0, wave_late[:, :, 1:-1, rows - 1], wave_late[:, :, 1:-1, 0])
    edge = lax.ppermute(edge, "radial", [(0, 1), (1, 0)])

    count, item, passed = pl.pallas_call(
        functools.partial(item_kernel, devices),
        out_shape=(
            jax.ShapeDtypeStruct((GROUPS,), jnp.int32),
            jax.ShapeDtypeStruct((GROUPS, ENTRIES), jnp.int32),
            jax.ShapeDtypeStruct((2,), jnp.int32),
        ),
        in_specs=[SMEM, HBM, HBM, SMEM, SMEM],
        out_specs=(SMEM,) * 3,
        scratch_shapes=[*index_scratch, dma(2)],
        compiler_params=params(4),
        cost_estimate=cost(6),
        name="item_kernel",
    )(me_late, sources, channel_slot, couple_pair, couple_order)

    fields = pl.pallas_call(
        field_kernel,
        out_shape=[jax.ShapeDtypeStruct((3 * ORDERS, rows, columns), jnp.float32)] * PLANES,
        in_specs=[SMEM],
        out_specs=[VMEM] * PLANES,
        compiler_params=params(16),
        cost_estimate=cost(2),
        name="field_kernel",
    )(behind(start_late, count))

    diag_step = pl.pallas_call(
        diagonal_kernel,
        grid=(HELD, 2),
        out_shape=jax.ShapeDtypeStruct((HELD, 2, PLANES, rows, columns), bf16),
        in_specs=[
            SMEM,
            SMEM,
            pl.BlockSpec((1, 1, PLANES + 2, rows, columns), lambda s, c: (s, c, 0, 0, 0)),
            pl.BlockSpec((1, 1, PLANES, columns), lambda s, c: (s, c, 0, 0)),
        ],
        out_specs=pl.BlockSpec((1, 1, PLANES, rows, columns), lambda s, c: (s, 1 - c, 0, 0, 0)),
        compiler_params=params(10),
        cost_estimate=cost(7),
        name="diagonal_kernel",
    )(behind(start_late, fields), l_values, wave, edge)

    fars, nears = [], []
    last = diag_step
    for p in range(PLANES):
        up, down = behind((ups[p], downs[p]), last)
        up_one, down_one, down_three, up_three = pl.pallas_call(
            pass_kernel,
            out_shape=(one,) * 4,
            in_specs=[SMEM, VMEM, VMEM],
            out_specs=(VMEM,) * 4,
            compiler_params=params(8),
            cost_estimate=cost(1),
            name="pass_kernel",
        )(passed, up, down)
        fars.append([v[None] for v in (shift(up_one, 1), shift(up_three, 3), shift(down_one, -1), shift(down_three, -3))])
        weights = behind(couple_weight, up_one)
        near = pl.pallas_call(
            functools.partial(near_kernel, p),
            out_shape=total,
            in_specs=[SMEM] * 3 + [HBM] + [VMEM] * 3,
            out_specs=VMEM,
            scratch_shapes=[pltpu.VMEM((HELD, 2, rows, columns), bf16), pltpu.SemaphoreType.DMA(())],
            compiler_params=params(12),
            cost_estimate=cost(3),
            name="near_kernel",
        )(count, item, weights, wave, up, down, fields[p])
        nears.append(near)
        last = near

    coupling = None
    for p in range(PLANES):
        inputs = [count, item, couple_weight, nears[p], *fars[p], fields[p]]
        specs = [SMEM] * 3 + [VMEM] * 6
        if p == 0:
            inputs[0] = behind(count, last)
        aliases = {}
        if coupling is not None:
            aliases = {len(inputs): 0}
            inputs.append(coupling)
            specs.append(ANY)
        coupling = pl.pallas_call(
            functools.partial(far_kernel, p),
            out_shape=jax.ShapeDtypeStruct((HELD, 2, PLANES, rows, columns), bf16),
            in_specs=specs,
            out_specs=ANY,
            scratch_shapes=[
                pltpu.VMEM(total.shape, total.dtype),
                pltpu.VMEM((HELD, 2, rows, columns), bf16),
                dma(HELD),
            ],
            input_output_aliases=aliases,
            compiler_params=params(12),
            cost_estimate=cost(2),
            name="far_kernel",
        )(*inputs)
    return diag_step, coupling


def solution(mesh):
    placed = (
        P("chan", None, None, "radial", None),
        P("chan", None),
        P(),
        P("chan", None),
        P("chan", None),
        P("chan", None),
        P(),
    )
    return jax.shard_map(
        shards,
        mesh=mesh,
        in_specs=placed,
        out_specs=(P("chan", None, None, "radial", None), P("chan", None, None, "radial", None)),
        check_vma=False,
    )
```

profile of v0, /device:TPU:0, one launch (start us, length us, event | category | flops | bytes accessed | tf_op | source)
XLA Modules:
  0.0 126.6 jit_solution(6460558172007929661)
XLA Ops:
  0.6 2.3 %copy-done = bf16[4,2,6,128,384]{4,3,2,1,0:T(8,128)(2,1)S(1)} copy-done((bf16[4,2,6,128,384]{4,3,2,1,0:T(8,128)(2,1)S(1)}, bf16[4,2,6,128,384]{4,3,2,1,0:T(8,128)(2,1)}, u32[]{:S(2)}) %copy-start) | copy-done | bytes 4718616
  4.4 3.7 %first_kernel.1 = (s32[6]{0:T(128)S(1)}, bf16[3,2,128,384]{3,2,1,0:T(8,128)(2,1)}, bf16[3,2,128,384]{3,2,1,0:T(8,128)(2,1)}) custom-call(s32[1]{0:T(128)} %bitcast.me_ref, s32[8,512]{1,0:T(8,128)S(1)} %bitcast.39, s32[512]{0:T(512)S(1)} %copy-done.4, bf16[4,2,6,128,384]{4,3,2,1,0:T(8,128)(2,1)S(1)} %copy-done), custom_call_target="tpu_custom_call" | custom-call | bytes 9000000 | tf_op jit(solution)/shard_map/first_kernel/pallas_call | solution.py:315
  8.2 8.8 %collective-permute-start.8 = (bf16[3,2,128,384]{3,2,1,0:T(8,128)(2,1)}, bf16[3,2,128,384]{3,2,1,0:T(8,128)(2,1)S(1)}, u32[]{:S(2)}, u32[]{:S(2)}) collective-permute-start(bf16[3,2,128,384]{3,2,1,0:T(8,128)(2,1)} %get-tuple-element.72), channel_id=1, source_target_pairs={{0,254},{2,0},{4,2},{6,4},{8,6},{10,8},{12,10},{14,12},{16,14},{18... | collective-permute-start | bytes 1769480 | tf_op jit(solution)/shard_map/ppermute | solution.py:313
  17.0 4.0 %rest_kernel.1 = (bf16[3,2,128,384]{3,2,1,0:T(8,128)(2,1)}, bf16[3,2,128,384]{3,2,1,0:T(8,128)(2,1)}, bf16[3,2,128,384]{3,2,1,0:T(8,128)(2,1)S(1)}, bf16[3,2,128...) custom-call(s32[6]{0:T(128)S(1)} %get-tuple-element.52.picks_ref, ...), custom_call_target="tpu_custom_call" | custom-call | bytes 6000000 | tf_op jit(solution)/shard_map/rest_kernel/pallas_call | solution.py:326
  21.0 0.8 copy-done.9
  21.8 0.8 copy-done.11
  22.7 7.5 %collective-permute-start.6 = (bf16[3,2,128,384]{3,2,1,0:T(8,128)(2,1)}, bf16[3,2,128,384]{3,2,1,0:T(8,128)(2,1)S(1)}, u32[]{:S(2)}, u32[]{:S(2)}) collective-permute-start(bf16[3,2,128,384]{3,2,1,0:T(8,128)(2,1)} %get-tuple-element.54), channel_id=1, source_target_pairs={{0,254},{2,0},{4,2},{6,4},{8,6},{10,8},{12,10},{14,12},{16,14},{18... | collective-permute-start | bytes 1769480 | tf_op jit(solution)/shard_map/ppermute | solution.py:313
  30.2 5.4 %copy.12 = bf16[4,2,6,128,384]{4,2,1,0,3:T(8,128)(2,1)S(1)} copy(bf16[4,2,6,128,384]{4,3,2,1,0:T(8,128)(2,1)} %wave_ref.13) | data formatting | bytes 9437184 | tf_op jit(solution)/shard_map/optimization_barrier | solution.py:293
  35.8 1.2 collective-permute-done.edge_ref
  37.0 7.4 %collective-permute-start.4 = (bf16[3,2,128,384]{3,2,1,0:T(8,128)(2,1)S(1)}, bf16[3,2,128,384]{3,2,1,0:T(8,128)(2,1)S(1)}, u32[]{:S(2)}, u32[]{:S(2)}) collective-permute-start(bf16[3,2,128,384]{3,2,1,0:T(8,128)(2,1)S(1)} %copy-done.10), channel_id=1, source_target_pairs={{0,254},{2,0},{4,2},{6,4},{8,6},{10,8},{12,10},{14,12},{16,14},{18... | collective-permute-start | bytes 1769480 | tf_op jit(solution)/shard_map/ppermute | solution.py:313
  44.5 7.5 %collective-permute-start.2 = (bf16[3,2,128,384]{3,2,1,0:T(8,128)(2,1)S(1)}, bf16[3,2,128,384]{3,2,1,0:T(8,128)(2,1)S(1)}, u32[]{:S(2)}, u32[]{:S(2)}) collective-permute-start(bf16[3,2,128,384]{3,2,1,0:T(8,128)(2,1)S(1)} %get-tuple-element.58), channel_id=1, source_target_pairs={{0,254},{2,0},{4,2},{6,4},{8,6},{10,8},{12,10},{14,12},{16,14},{18... | collective-permute-start | bytes 1769480 | tf_op jit(solution)/shard_map/ppermute | solution.py:313
  51.9 6.7 %item_kernel.1 = (s32[7]{0:T(128)S(1)}, s32[7,32]{1,0:T(8,128)S(1)}, s32[2]{0:T(128)S(1)}) custom-call(s32[1]{0:T(128)} %bitcast.me_ref, s32[8,512]{1,0:T(8,128)S(1)} %bitcast.40, s32[512]{0:T(512)S(1)} %copy-done.5, s32[4,8]{1,0:T(4,128)S(1)} %copy-done.6, s32[4,8]{1,0:T(4,128)S(1)} %copy-done.7), custom_call_target="tpu_custom_call" | custom-call | bytes 18000000 | tf_op jit(solution)/shard_map/item_kernel/pallas_call | solution.py:343
  59.4 7.3 %diagonal_kernel.1 = bf16[4,2,4,128,384]{4,3,2,1,0:T(8,128)(2,1)} custom-call(s32[1]{0:T(128)} %bitcast.1.row_ref, s32[4,3]{1,0:T(4,128)S(1)} %copy-done.8, bf16[4,2,6,128,384]{4,3,2,1,0:T(8,128)(2,1)S(1)} %bitcast.22, bf16[4,2,4,384]{3,2,1,0:T(4,128)(2,1)S(1)} %collective-permute-done.edge_ref), custom_call_target="tpu_custom_call" | custom-call | bytes 21000000 | tf_op jit(solution)/shard_map/diagonal_kernel/pallas_call | solution.py:368
  67.4 2.9 %near_kernel.4.near = f32[4,2,128,384]{3,2,1,0:T(8,128)S(1)} custom-call(s32[7]{0:T(128)S(1)} %get-tuple-element.98.count_ref, s32[7,32]{1,0:T(8,128)S(1)} %get-tuple-element.69.item_ref, f32[4,8]{1,0:T(4,128)S(1)} %copy-done.1, bf16[4,2,6,128,384]{4,3,2,1,0:T(8,128)(2,1)S(1)} %bitcast.22, bf16[3,2,128,384]{3,2,1,0:T(8,128)(2,1)S(1)} %collective-permute-done.7.up_ref, ...), custom_call_target="tpu_custom_call" | custom-call | bytes 9000000 | tf_op jit(solution)/shard_map/near_kernel/pallas_call | solution.py:399
  71.2 6.4 %collective-permute-start.24 = (bf16[2,128,384]{2,1,0:T(8,128)(2,1)S(1)}, bf16[2,128,384]{2,1,0:T(8,128)(2,1)S(1)}, u32[]{:S(2)}, u32[]{:S(2)}) collective-permute-start(bf16[2,128,384]{2,1,0:T(8,128)(2,1)S(1)} %get-tuple-element.101), channel_id=1, source_target_pairs={{0,250},{2,252},{4,254},{6,0},{8,2},{10,4},{12,6},{14,8},{16,10},{... | collective-permute-start | bytes 589832 | tf_op jit(solution)/shard_map/ppermute | solution.py:313
  77.6 1.9 %collective-permute-start.21 = (bf16[2,128,384]{2,1,0:T(8,128)(2,1)S(1)}, bf16[2,128,384]{2,1,0:T(8,128)(2,1)S(1)}, u32[]{:S(2)}, u32[]{:S(2)}) collective-permute-start(bf16[2,128,384]{2,1,0:T(8,128)(2,1)S(1)} %get-tuple-element.75), channel_id=1, source_target_pairs={{0,2},{2,4},{4,6},{6,8},{8,10},{10,12},{12,14},{14,16},{16,18},{18... | collective-permute-start | bytes 589832 | tf_op jit(solution)/shard_map/ppermute | solution.py:313
  79.5 6.5 %collective-permute-start.19 = (bf16[2,128,384]{2,1,0:T(8,128)(2,1)S(1)}, bf16[2,128,384]{2,1,0:T(8,128)(2,1)S(1)}, u32[]{:S(2)}, u32[]{:S(2)}) collective-permute-start(bf16[2,128,384]{2,1,0:T(8,128)(2,1)S(1)} %get-tuple-element.96), channel_id=1, source_target_pairs={{0,254},{2,0},{4,2},{6,4},{8,6},{10,8},{12,10},{14,12},{16,14},{18... | collective-permute-start | bytes 589832 | tf_op jit(solution)/shard_map/ppermute | solution.py:313
  86.1 2.7 %near_kernel.5.near = f32[4,2,128,384]{3,2,1,0:T(8,128)S(1)} custom-call(s32[7]{0:T(128)S(1)} %get-tuple-element.98.count_ref, s32[7,32]{1,0:T(8,128)S(1)} %get-tuple-element.69.item_ref, f32[4,8]{1,0:T(4,128)S(1)} %copy-done.1, bf16[4,2,6,128,384]{4,3,2,1,0:T(8,128)(2,1)S(1)} %bitcast.22, bf16[3,2,128,384]{3,2,1,0:T(8,128)(2,1)S(1)} %collective-permute-done.5.up_ref, ...), custom_call_target="tpu_custom_call" | custom-call | bytes 9000000 | tf_op jit(solution)/shard_map/near_kernel/pallas_call | solution.py:399
  89.4 1.3 %collective-permute-start.20 = (bf16[2,128,384]{2,1,0:T(8,128)(2,1)S(1)}, bf16[2,128,384]{2,1,0:T(8,128)(2,1)S(1)}, u32[]{:S(2)}, u32[]{:S(2)}) collective-permute-start(bf16[2,128,384]{2,1,0:T(8,128)(2,1)S(1)} %get-tuple-element.97), channel_id=1, source_target_pairs={{0,250},{2,252},{4,254},{6,0},{8,2},{10,4},{12,6},{14,8},{16,10},{... | collective-permute-start | bytes 589832 | tf_op jit(solution)/shard_map/ppermute | solution.py:313
  91.3 1.5 %collective-permute-start.14 = (bf16[2,128,384]{2,1,0:T(8,128)(2,1)S(1)}, bf16[2,128,384]{2,1,0:T(8,128)(2,1)S(1)}, u32[]{:S(2)}, u32[]{:S(2)}) collective-permute-start(bf16[2,128,384]{2,1,0:T(8,128)(2,1)S(1)} %get-tuple-element.92), channel_id=1, source_target_pairs={{0,6},{2,8},{4,10},{6,12},{8,14},{10,16},{12,18},{14,20},{16,22},{... | collective-permute-start | bytes 589832 | tf_op jit(solution)/shard_map/ppermute | solution.py:313
  92.8 6.2 %collective-permute-start.15 = (bf16[2,128,384]{2,1,0:T(8,128)(2,1)S(1)}, bf16[2,128,384]{2,1,0:T(8,128)(2,1)S(1)}, u32[]{:S(2)}, u32[]{:S(2)}) collective-permute-start(bf16[2,128,384]{2,1,0:T(8,128)(2,1)S(1)} %get-tuple-element.93), channel_id=1, source_target_pairs={{0,254},{2,0},{4,2},{6,4},{8,6},{10,8},{12,10},{14,12},{16,14},{18... | collective-permute-start | bytes 589832 | tf_op jit(solution)/shard_map/ppermute | solution.py:313
  99.0 1.2 collective-permute-start.16
  100.2 2.8 %near_kernel.6.near = f32[4,2,128,384]{3,2,1,0:T(8,128)S(1)} custom-call(s32[7]{0:T(128)S(1)} %get-tuple-element.98.count_ref, s32[7,32]{1,0:T(8,128)S(1)} %get-tuple-element.69.item_ref, f32[4,8]{1,0:T(4,128)S(1)} %copy-done.1, bf16[4,2,6,128,384]{4,3,2,1,0:T(8,128)(2,1)S(1)} %bitcast.22, bf16[3,2,128,384]{3,2,1,0:T(8,128)(2,1)S(1)} %collective-permute-done.3.up_ref, ...), custom_call_target="tpu_custom_call" | custom-call | bytes 9000000 | tf_op jit(solution)/shard_map/near_kernel/pallas_call | solution.py:399
  104.0 1.7 %collective-permute-start.10 = (bf16[2,128,384]{2,1,0:T(8,128)(2,1)S(1)}, bf16[2,128,384]{2,1,0:T(8,128)(2,1)S(1)}, u32[]{:S(2)}, u32[]{:S(2)}) collective-permute-start(bf16[2,128,384]{2,1,0:T(8,128)(2,1)S(1)} %get-tuple-element.89), channel_id=1, source_target_pairs={{0,6},{2,8},{4,10},{6,12},{8,14},{10,16},{12,18},{14,20},{16,22},{... | collective-permute-start | bytes 589832 | tf_op jit(solution)/shard_map/ppermute | solution.py:313
  105.7 6.1 %collective-permute-start.11 = (bf16[2,128,384]{2,1,0:T(8,128)(2,1)S(1)}, bf16[2,128,384]{2,1,0:T(8,128)(2,1)S(1)}, u32[]{:S(2)}, u32[]{:S(2)}) collective-permute-start(bf16[2,128,384]{2,1,0:T(8,128)(2,1)S(1)} %get-tuple-element.90), channel_id=1, source_target_pairs={{0,254},{2,0},{4,2},{6,4},{8,6},{10,8},{12,10},{14,12},{16,14},{18... | collective-permute-start | bytes 589832 | tf_op jit(solution)/shard_map/ppermute | solution.py:313
  111.9 1.3 %collective-permute-start.12 = (bf16[2,128,384]{2,1,0:T(8,128)(2,1)S(1)}, bf16[2,128,384]{2,1,0:T(8,128)(2,1)S(1)}, u32[]{:S(2)}, u32[]{:S(2)}) collective-permute-start(bf16[2,128,384]{2,1,0:T(8,128)(2,1)S(1)} %get-tuple-element.91), channel_id=1, source_target_pairs={{0,250},{2,252},{4,254},{6,0},{8,2},{10,4},{12,6},{14,8},{16,10},{... | collective-permute-start | bytes 589832 | tf_op jit(solution)/shard_map/ppermute | solution.py:313
  113.2 2.8 %near_kernel.7.near = f32[4,2,128,384]{3,2,1,0:T(8,128)S(1)} custom-call(s32[7]{0:T(128)S(1)} %get-tuple-element.98.count_ref, s32[7,32]{1,0:T(8,128)S(1)} %get-tuple-element.69.item_ref, f32[4,8]{1,0:T(4,128)S(1)} %copy-done.1, bf16[4,2,6,128,384]{4,3,2,1,0:T(8,128)(2,1)S(1)} %bitcast.22, bf16[3,2,128,384]{3,2,1,0:T(8,128)(2,1)S(1)} %collective-permute-done.1.up_ref, ...), custom_call_target="tpu_custom_call" | custom-call | bytes 9000000 | tf_op jit(solution)/shard_map/near_kernel/pallas_call | solution.py:399
  116.0 2.1 %far_kernel.4.refs_5_ = bf16[4,2,4,128,384]{4,3,2,1,0:T(8,128)(2,1)} custom-call(s32[7]{0:T(128)S(1)} %get-tuple-element.98.count_ref, s32[7,32]{1,0:T(8,128)S(1)} %get-tuple-element.69.item_ref, f32[4,8]{1,0:T(4,128)S(1)} %copy-done.1, f32[4,2,128,384]{3,2,1,0:T(8,128)S(1)} %near_kernel.4.near, bf16[1,2,128,384]{3,2,1,0:T(8,128)(2,1)S(1)} %bitcast.26, ...), custom_call_target="tpu_custom_call" | custom-call | bytes 6000000 | tf_op jit(solution)/shard_map/far_kernel/pallas_call | solution.py:423
  118.1 2.1 %far_kernel.5.refs_5_ = bf16[4,2,4,128,384]{4,3,2,1,0:T(8,128)(2,1)} custom-call(s32[7]{0:T(128)S(1)} %get-tuple-element.98.count_ref, s32[7,32]{1,0:T(8,128)S(1)} %get-tuple-element.69.item_ref, f32[4,8]{1,0:T(4,128)S(1)} %copy-done.1, f32[4,2,128,384]{3,2,1,0:T(8,128)S(1)} %near_kernel.5.near, ...), custom_call_target="tpu_custom_call", output_to_operand_aliasing={{}: (9, {})} | custom-call | bytes 6000000 | tf_op jit(solution)/shard_map/far_kernel/pallas_call | solution.py:423
  120.3 2.2 %far_kernel.6.refs_5_ = bf16[4,2,4,128,384]{4,3,2,1,0:T(8,128)(2,1)} custom-call(s32[7]{0:T(128)S(1)} %get-tuple-element.98.count_ref, s32[7,32]{1,0:T(8,128)S(1)} %get-tuple-element.69.item_ref, f32[4,8]{1,0:T(4,128)S(1)} %copy-done.1, f32[4,2,128,384]{3,2,1,0:T(8,128)S(1)} %near_kernel.6.near, ...), custom_call_target="tpu_custom_call", output_to_operand_aliasing={{}: (9, {})} | custom-call | bytes 6000000 | tf_op jit(solution)/shard_map/far_kernel/pallas_call | solution.py:423
  122.5 1.8 %collective-permute-done.9 = bf16[2,128,384]{2,1,0:T(8,128)(2,1)S(1)} collective-permute-done((bf16[2,128,384]{2,1,0:T(8,128)(2,1)S(1)}, bf16[2,128,384]{2,1,0:T(8,128)(2,1)S(1)}, u32[]{:S(2)}, u32[]{:S(2)}) %collective-permute-start.9) | collective-permute-done | bytes 196640 | tf_op jit(solution)/shard_map/ppermute | solution.py:313
  124.3 2.1 %far_kernel.7 = bf16[4,2,4,128,384]{4,3,2,1,0:T(8,128)(2,1)} custom-call(s32[7]{0:T(128)S(1)} %get-tuple-element.98.count_ref, s32[7,32]{1,0:T(8,128)S(1)} %get-tuple-element.69.item_ref, f32[4,8]{1,0:T(4,128)S(1)} %copy-done.1, f32[4,2,128,384]{3,2,1,0:T(8,128)S(1)} %near_kernel.7.near, ...), custom_call_target="tpu_custom_call", output_to_operand_aliasing={{}: (9, {})} | custom-call | bytes 6000000 | tf_op jit(solution)/shard_map/far_kernel/pallas_call | solution.py:423
  (68 shorter events, 6.2 us)
Async XLA Ops:
  8.1 28.9 %collective-permute-start.7 = (bf16[3,2,128,384]{3,2,1,0:T(8,128)(2,1)}, bf16[3,2,128,384]{3,2,1,0:T(8,128)(2,1)S(1)}, u32[]{:S(2)}, u32[]{:S(2)}) collective-permute-start(bf16[3,2,128,384]{3,2,1,0:T(8,128)(2,1)} %get-tuple-element.71), channel_id=1, source_target_pairs={{0,2},{2,4},{4,6},{6,8},{8,10},{10,12},{12,14},{14,16},{16,18},{18... | collective-permute-start | bytes 1769480 | tf_op jit(solution)/shard_map/ppermute | solution.py:313
  8.2 36.3 %collective-permute-start.8 = (bf16[3,2,128,384]{3,2,1,0:T(8,128)(2,1)}, bf16[3,2,128,384]{3,2,1,0:T(8,128)(2,1)S(1)}, u32[]{:S(2)}, u32[]{:S(2)}) collective-permute-start(bf16[3,2,128,384]{3,2,1,0:T(8,128)(2,1)} %get-tuple-element.72), channel_id=1, source_target_pairs={{0,254},{2,0},{4,2},{6,4},{8,6},{10,8},{12,10},{14,12},{16,14},{18... | collective-permute-start | bytes 1769480 | tf_op jit(solution)/shard_map/ppermute | solution.py:313
  22.7 21.8 %collective-permute-start.5 = (bf16[3,2,128,384]{3,2,1,0:T(8,128)(2,1)}, bf16[3,2,128,384]{3,2,1,0:T(8,128)(2,1)S(1)}, u32[]{:S(2)}, u32[]{:S(2)}) collective-permute-start(bf16[3,2,128,384]{3,2,1,0:T(8,128)(2,1)} %get-tuple-element.53), channel_id=1, source_target_pairs={{0,2},{2,4},{4,6},{6,8},{8,10},{10,12},{12,14},{14,16},{16,18},{18... | collective-permute-start | bytes 1769480 | tf_op jit(solution)/shard_map/ppermute | solution.py:313
  22.7 44.6 %collective-permute-start.6 = (bf16[3,2,128,384]{3,2,1,0:T(8,128)(2,1)}, bf16[3,2,128,384]{3,2,1,0:T(8,128)(2,1)S(1)}, u32[]{:S(2)}, u32[]{:S(2)}) collective-permute-start(bf16[3,2,128,384]{3,2,1,0:T(8,128)(2,1)} %get-tuple-element.54), channel_id=1, source_target_pairs={{0,254},{2,0},{4,2},{6,4},{8,6},{10,8},{12,10},{14,12},{16,14},{18... | collective-permute-start | bytes 1769480 | tf_op jit(solution)/shard_map/ppermute | solution.py:313
  30.1 29.2 %slice-start = ((s8[4718592]{0:T(1024)(128)(4,1)}), s8[4194304]{0:T(1024)(128)(4,1)S(1)}, s32[]{:S(2)}) async-start(s8[4718592]{0:T(1024)(128)(4,1)} %bitcast.21), calls=%async_computation | async-start | bytes 8388608
  30.1 21.8 %copy-start.3 = (s32[512,8]{0,1:T(8,128)S(1)}, s32[512,8]{0,1:T(8,128)}, u32[]{:S(2)}) copy-start(s32[512,8]{0,1:T(8,128)} %param.9) | copy-start | bytes 49156
  30.1 21.8 %copy-start.5 = (s32[512]{0:T(512)S(1)}, s32[512]{0:T(512)}, u32[]{:S(2)}) copy-start(s32[512]{0:T(512)} %slots.3) | copy-start | bytes 6148
  30.2 21.8 %copy-start.6 = (s32[4,8]{1,0:T(4,128)S(1)}, s32[4,8]{1,0:T(4,128)}, u32[]{:S(2)}) copy-start(s32[4,8]{1,0:T(4,128)} %pair_ref.1) | copy-start | bytes 388
  30.2 21.8 %copy-start.7 = (s32[4,8]{1,0:T(4,128)S(1)}, s32[4,8]{1,0:T(4,128)}, u32[]{:S(2)}) copy-start(s32[4,8]{1,0:T(4,128)} %order_ref.1) | copy-start | bytes 388
  30.2 29.2 %slice-start.1 = ((s8[4718592]{0:T(1024)(128)(4,1)}), s8[524288]{0:T(1024)(128)(4,1)S(1)}, s32[]{:S(2)}) async-start(s8[4718592]{0:T(1024)(128)(4,1)} %bitcast.21), calls=%async_computation.1 | async-start | bytes 1048576
  30.2 29.2 %copy-start.8 = (s32[4,3]{1,0:T(4,128)S(1)}, s32[4,3]{1,0:T(4,128)}, u32[]{:S(2)}) copy-start(s32[4,3]{1,0:T(4,128)} %l_ref.1) | copy-start | bytes 148
  35.7 1.3 %collective-permute-start = (bf16[4,2,4,384]{3,2,1,0:T(4,128)(2,1)S(1)}, bf16[4,2,4,384]{3,2,1,0:T(4,128)(2,1)S(1)}, u32[]{:S(2)}, u32[]{:S(2)}) collective-permute-start(bf16[4,2,4,384]{3,2,1,0:T(4,128)(2,1)S(1)} %fusion), channel_id=1, source_target_pairs={{0,1},{1,0},{2,3},{3,2},{4,5},{5,4},{6,7},{7,6},{8,9},{9,8},{10,11... | collective-permute-start | bytes 73736 | tf_op jit(solution)/shard_map/ppermute | solution.py:341
  37.0 33.9 %collective-permute-start.3 = (bf16[3,2,128,384]{3,2,1,0:T(8,128)(2,1)S(1)}, bf16[3,2,128,384]{3,2,1,0:T(8,128)(2,1)S(1)}, u32[]{:S(2)}, u32[]{:S(2)}) collective-permute-start(bf16[3,2,128,384]{3,2,1,0:T(8,128)(2,1)S(1)} %copy-done.12), channel_id=1, source_target_pairs={{0,2},{2,4},{4,6},{6,8},{8,10},{10,12},{12,14},{14,16},{16,18},{18... | collective-permute-start | bytes 1769480 | tf_op jit(solution)/shard_map/ppermute | solution.py:313
  37.0 34.2 %collective-permute-start.4 = (bf16[3,2,128,384]{3,2,1,0:T(8,128)(2,1)S(1)}, bf16[3,2,128,384]{3,2,1,0:T(8,128)(2,1)S(1)}, u32[]{:S(2)}, u32[]{:S(2)}) collective-permute-start(bf16[3,2,128,384]{3,2,1,0:T(8,128)(2,1)S(1)} %copy-done.10), channel_id=1, source_target_pairs={{0,254},{2,0},{4,2},{6,4},{8,6},{10,8},{12,10},{14,12},{16,14},{18... | collective-permute-start | bytes 1769480 | tf_op jit(solution)/shard_map/ppermute | solution.py:313
  44.4 33.1 %collective-permute-start.1 = (bf16[3,2,128,384]{3,2,1,0:T(8,128)(2,1)S(1)}, bf16[3,2,128,384]{3,2,1,0:T(8,128)(2,1)S(1)}, u32[]{:S(2)}, u32[]{:S(2)}) collective-permute-start(bf16[3,2,128,384]{3,2,1,0:T(8,128)(2,1)S(1)} %get-tuple-element.57), channel_id=1, source_target_pairs={{0,2},{2,4},{4,6},{6,8},{8,10},{10,12},{12,14},{14,16},{16,18},{18... | collective-permute-start | bytes 1769480 | tf_op jit(solution)/shard_map/ppermute | solution.py:313
  44.5 35.0 %collective-permute-start.2 = (bf16[3,2,128,384]{3,2,1,0:T(8,128)(2,1)S(1)}, bf16[3,2,128,384]{3,2,1,0:T(8,128)(2,1)S(1)}, u32[]{:S(2)}, u32[]{:S(2)}) collective-permute-start(bf16[3,2,128,384]{3,2,1,0:T(8,128)(2,1)S(1)} %get-tuple-element.58), channel_id=1, source_target_pairs={{0,254},{2,0},{4,2},{6,4},{8,6},{10,8},{12,10},{14,12},{16,14},{18... | collective-permute-start | bytes 1769480 | tf_op jit(solution)/shard_map/ppermute | solution.py:313
  67.3 12.2 %collective-permute-start.22 = (bf16[2,128,384]{2,1,0:T(8,128)(2,1)S(1)}, bf16[2,128,384]{2,1,0:T(8,128)(2,1)S(1)}, u32[]{:S(2)}, u32[]{:S(2)}) collective-permute-start(bf16[2,128,384]{2,1,0:T(8,128)(2,1)S(1)} %get-tuple-element.99), channel_id=1, source_target_pairs={{0,6},{2,8},{4,10},{6,12},{8,14},{10,16},{12,18},{14,20},{16,22},{... | collective-permute-start | bytes 589832 | tf_op jit(solution)/shard_map/ppermute | solution.py:313
  70.9 18.5 %collective-permute-start.23 = (bf16[2,128,384]{2,1,0:T(8,128)(2,1)S(1)}, bf16[2,128,384]{2,1,0:T(8,128)(2,1)S(1)}, u32[]{:S(2)}, u32[]{:S(2)}) collective-permute-start(bf16[2,128,384]{2,1,0:T(8,128)(2,1)S(1)} %get-tuple-element.100), channel_id=1, source_target_pairs={{0,254},{2,0},{4,2},{6,4},{8,6},{10,8},{12,10},{14,12},{16,14},{18... | collective-permute-start | bytes 589832 | tf_op jit(solution)/shard_map/ppermute | solution.py:313
  71.2 19.6 %collective-permute-start.24 = (bf16[2,128,384]{2,1,0:T(8,128)(2,1)S(1)}, bf16[2,128,384]{2,1,0:T(8,128)(2,1)S(1)}, u32[]{:S(2)}, u32[]{:S(2)}) collective-permute-start(bf16[2,128,384]{2,1,0:T(8,128)(2,1)S(1)} %get-tuple-element.101), channel_id=1, source_target_pairs={{0,250},{2,252},{4,254},{6,0},{8,2},{10,4},{12,6},{14,8},{16,10},{... | collective-permute-start | bytes 589832 | tf_op jit(solution)/shard_map/ppermute | solution.py:313
  77.6 13.7 %collective-permute-start.21 = (bf16[2,128,384]{2,1,0:T(8,128)(2,1)S(1)}, bf16[2,128,384]{2,1,0:T(8,128)(2,1)S(1)}, u32[]{:S(2)}, u32[]{:S(2)}) collective-permute-start(bf16[2,128,384]{2,1,0:T(8,128)(2,1)S(1)} %get-tuple-element.75), channel_id=1, source_target_pairs={{0,2},{2,4},{4,6},{6,8},{8,10},{10,12},{12,14},{14,16},{16,18},{18... | collective-permute-start | bytes 589832 | tf_op jit(solution)/shard_map/ppermute | solution.py:313
  79.5 13.3 %collective-permute-start.18 = (bf16[2,128,384]{2,1,0:T(8,128)(2,1)S(1)}, bf16[2,128,384]{2,1,0:T(8,128)(2,1)S(1)}, u32[]{:S(2)}, u32[]{:S(2)}) collective-permute-start(bf16[2,128,384]{2,1,0:T(8,128)(2,1)S(1)} %get-tuple-element.95), channel_id=1, source_target_pairs={{0,6},{2,8},{4,10},{6,12},{8,14},{10,16},{12,18},{14,20},{16,22},{... | collective-permute-start | bytes 589832 | tf_op jit(solution)/shard_map/ppermute | solution.py:313
  79.5 19.5 %collective-permute-start.19 = (bf16[2,128,384]{2,1,0:T(8,128)(2,1)S(1)}, bf16[2,128,384]{2,1,0:T(8,128)(2,1)S(1)}, u32[]{:S(2)}, u32[]{:S(2)}) collective-permute-start(bf16[2,128,384]{2,1,0:T(8,128)(2,1)S(1)} %get-tuple-element.96), channel_id=1, source_target_pairs={{0,254},{2,0},{4,2},{6,4},{8,6},{10,8},{12,10},{14,12},{16,14},{18... | collective-permute-start | bytes 589832 | tf_op jit(solution)/shard_map/ppermute | solution.py:313
  89.4 14.2 %collective-permute-start.20 = (bf16[2,128,384]{2,1,0:T(8,128)(2,1)S(1)}, bf16[2,128,384]{2,1,0:T(8,128)(2,1)S(1)}, u32[]{:S(2)}, u32[]{:S(2)}) collective-permute-start(bf16[2,128,384]{2,1,0:T(8,128)(2,1)S(1)} %get-tuple-element.97), channel_id=1, source_target_pairs={{0,250},{2,252},{4,254},{6,0},{8,2},{10,4},{12,6},{14,8},{16,10},{... | collective-permute-start | bytes 589832 | tf_op jit(solution)/shard_map/ppermute | solution.py:313
  90.7 13.3 %collective-permute-start.17 = (bf16[2,128,384]{2,1,0:T(8,128)(2,1)S(1)}, bf16[2,128,384]{2,1,0:T(8,128)(2,1)S(1)}, u32[]{:S(2)}, u32[]{:S(2)}) collective-permute-start(bf16[2,128,384]{2,1,0:T(8,128)(2,1)S(1)} %get-tuple-element.79), channel_id=1, source_target_pairs={{0,2},{2,4},{4,6},{6,8},{8,10},{10,12},{12,14},{14,16},{16,18},{18... | collective-permute-start | bytes 589832 | tf_op jit(solution)/shard_map/ppermute | solution.py:313
  91.3 14.5 %collective-permute-start.14 = (bf16[2,128,384]{2,1,0:T(8,128)(2,1)S(1)}, bf16[2,128,384]{2,1,0:T(8,128)(2,1)S(1)}, u32[]{:S(2)}, u32[]{:S(2)}) collective-permute-start(bf16[2,128,384]{2,1,0:T(8,128)(2,1)S(1)} %get-tuple-element.92), channel_id=1, source_target_pairs={{0,6},{2,8},{4,10},{6,12},{8,14},{10,16},{12,18},{14,20},{16,22},{... | collective-permute-start | bytes 589832 | tf_op jit(solution)/shard_map/ppermute | solution.py:313
  92.8 19.1 %collective-permute-start.15 = (bf16[2,128,384]{2,1,0:T(8,128)(2,1)S(1)}, bf16[2,128,384]{2,1,0:T(8,128)(2,1)S(1)}, u32[]{:S(2)}, u32[]{:S(2)}) collective-permute-start(bf16[2,128,384]{2,1,0:T(8,128)(2,1)S(1)} %get-tuple-element.93), channel_id=1, source_target_pairs={{0,254},{2,0},{4,2},{6,4},{8,6},{10,8},{12,10},{14,12},{16,14},{18... | collective-permute-start | bytes 589832 | tf_op jit(solution)/shard_map/ppermute | solution.py:313
  99.0 14.2 %collective-permute-start.16 = (bf16[2,128,384]{2,1,0:T(8,128)(2,1)S(1)}, bf16[2,128,384]{2,1,0:T(8,128)(2,1)S(1)}, u32[]{:S(2)}, u32[]{:S(2)}) collective-permute-start(bf16[2,128,384]{2,1,0:T(8,128)(2,1)S(1)} %get-tuple-element.94), channel_id=1, source_target_pairs={{0,250},{2,252},{4,254},{6,0},{8,2},{10,4},{12,6},{14,8},{16,10},{... | collective-permute-start | bytes 589832 | tf_op jit(solution)/shard_map/ppermute | solution.py:313
  103.6 16.7 %collective-permute-start.13 = (bf16[2,128,384]{2,1,0:T(8,128)(2,1)S(1)}, bf16[2,128,384]{2,1,0:T(8,128)(2,1)S(1)}, u32[]{:S(2)}, u32[]{:S(2)}) collective-permute-start(bf16[2,128,384]{2,1,0:T(8,128)(2,1)S(1)} %get-tuple-element.83), channel_id=1, source_target_pairs={{0,2},{2,4},{4,6},{6,8},{8,10},{10,12},{12,14},{14,16},{16,18},{18... | collective-permute-start | bytes 589832 | tf_op jit(solution)/shard_map/ppermute | solution.py:313
  104.0 18.5 %collective-permute-start.10 = (bf16[2,128,384]{2,1,0:T(8,128)(2,1)S(1)}, bf16[2,128,384]{2,1,0:T(8,128)(2,1)S(1)}, u32[]{:S(2)}, u32[]{:S(2)}) collective-permute-start(bf16[2,128,384]{2,1,0:T(8,128)(2,1)S(1)} %get-tuple-element.89), channel_id=1, source_target_pairs={{0,6},{2,8},{4,10},{6,12},{8,14},{10,16},{12,18},{14,20},{16,22},{... | collective-permute-start | bytes 589832 | tf_op jit(solution)/shard_map/ppermute | solution.py:313
  105.7 16.8 %collective-permute-start.11 = (bf16[2,128,384]{2,1,0:T(8,128)(2,1)S(1)}, bf16[2,128,384]{2,1,0:T(8,128)(2,1)S(1)}, u32[]{:S(2)}, u32[]{:S(2)}) collective-permute-start(bf16[2,128,384]{2,1,0:T(8,128)(2,1)S(1)} %get-tuple-element.90), channel_id=1, source_target_pairs={{0,254},{2,0},{4,2},{6,4},{8,6},{10,8},{12,10},{14,12},{16,14},{18... | collective-permute-start | bytes 589832 | tf_op jit(solution)/shard_map/ppermute | solution.py:313
  111.9 10.6 %collective-permute-start.12 = (bf16[2,128,384]{2,1,0:T(8,128)(2,1)S(1)}, bf16[2,128,384]{2,1,0:T(8,128)(2,1)S(1)}, u32[]{:S(2)}, u32[]{:S(2)}) collective-permute-start(bf16[2,128,384]{2,1,0:T(8,128)(2,1)S(1)} %get-tuple-element.91), channel_id=1, source_target_pairs={{0,250},{2,252},{4,254},{6,0},{8,2},{10,4},{12,6},{14,8},{16,10},{... | collective-permute-start | bytes 589832 | tf_op jit(solution)/shard_map/ppermute | solution.py:313
  113.2 11.1 %collective-permute-start.9 = (bf16[2,128,384]{2,1,0:T(8,128)(2,1)S(1)}, bf16[2,128,384]{2,1,0:T(8,128)(2,1)S(1)}, u32[]{:S(2)}, u32[]{:S(2)}) collective-permute-start(bf16[2,128,384]{2,1,0:T(8,128)(2,1)S(1)} %get-tuple-element.87), channel_id=1, source_target_pairs={{0,2},{2,4},{4,6},{6,8},{8,10},{10,12},{12,14},{14,16},{16,18},{18... | collective-permute-start | bytes 589832 | tf_op jit(solution)/shard_map/ppermute | solution.py:313
  (8 other events, 27.1 us)
where the time goes:
time: 127 us
  starting transfers between devices  66.6 us (52%)
  Pallas kernels  44.6 us (35%)
  local copies, waits for them, and re-layouts  10.9 us (9%)
  waiting for transfers between devices  3.28 us (3%)
    ppermute x24, starting transfers between devices, shift(): lax.ppermute(array, 'chan', [(i, (i + by) % devices) for i in range(devic...  66.6 us
    pallas_call x4, Pallas kernels, shards(): pl.pallas_call(functools.partial(near_kernel, p), out_shape=total, in_spe...  11.2 us
    pallas_call x4, Pallas kernels, shards(): pl.pallas_call(functools.partial(far_kernel, p), out_shape=jax.ShapeDtype...  8.63 us
    pallas_call x1, Pallas kernels, shards(): pl.pallas_call(diagonal_kernel, grid=(HELD, 2), out_shape=jax.ShapeDtypeS...  7.28 us
    pallas_call x1, Pallas kernels, shards(): pl.pallas_call(functools.partial(item_kernel, devices), out_shape=(jax.Sh...  6.68 us
    optimization_barrier x1, local copies, waits for them, and re-layouts, behind(): return lax.optimization_barrier((value, others))[0]  5.44 us
    unnamed x30, local copies, waits for them, and re-layouts  5.42 us
    pallas_call x1, Pallas kernels, shards(): pl.pallas_call(functools.partial(rest_kernel, later), out_shape=[message]...  4.03 us
  transfers between devices with their start and end apart: 25, of which 3 were waited for; matrix products, arithmetic and copies ran while one was open for 4% of the time, Pallas kernels for 31%

commit v1 on v0

v1 whole, which is shorter than its diff:
```python
import functools

import jax
import jax.numpy as jnp
from jax import lax
from jax.experimental import pallas as pl
from jax.experimental.pallas import tpu as pltpu
from jax.sharding import PartitionSpec as P

WSTART = 16
grid_step = 0.25
charge = 3.0
time_step = 0.02

HELD = 4
PARTS = 8
PLANES = 4
HALF = 2
EDGE = 16
ORDERS = 4
ENTRIES = HELD * PARTS
GROUPS = 5

PAIR_LOW = 1233667140
PAIR_HIGH = 1234062796


def two_of(mask):
    word = jnp.where(mask >= 8, PAIR_HIGH, PAIR_LOW)
    code = lax.shift_right_logical(word, 4 * (mask & 7)) & 15
    return code & 3, code >> 2


def needed(source_ref, slot_ref, device, offset, devices):
    reader = device + offset
    inside = (reader >= 0) & (reader < devices)
    row = jnp.clip(reader, 0, devices - 1) * HELD
    mask = jnp.int32(0)
    for i in range(HELD):
        for e in range(PARTS):
            slot = slot_ref[source_ref[e, row + i]]
            mask = mask | jnp.where(slot // HELD == device, jnp.int32(1) << (slot % HELD), 0)
    return two_of(jnp.where(inside, mask, 0))


def run(copies):
    for copy in copies:
        copy.start()
    for copy in copies:
        copy.wait()


def head_kernel(wave_ref, up_ref, down_ref, up_held, down_held, in_sem, out_sem):
    steps = []
    for s in range(HELD):
        for ref, held, start in ((up_ref, up_held, 0), (down_ref, down_held, HALF)):
            n = len(steps)
            steps.append((
                pltpu.make_async_copy(wave_ref.at[s, :, pl.ds(1 + start, HALF)], held.at[s], in_sem.at[n]),
                pltpu.make_async_copy(held.at[s], ref.at[s], out_sem.at[n]),
            ))
    for come, _ in steps:
        come.start()
    for come, go in steps:
        come.wait()
        go.start()
    for _, go in steps:
        go.wait()


def select_kernel(
    devices,
    edge_rows,
    me_ref,
    core_ref,
    sources,
    slots,
    wave_ref,
    up_ref,
    down_ref,
    edge_ref,
    source_ref,
    slot_ref,
    sem,
):
    rows = wave_ref.shape[3]
    at = pl.multiple_of((1 - core_ref[0]) * (rows - edge_rows), edge_rows)
    edge = pltpu.make_async_copy(
        wave_ref.at[:, :, pl.ds(1, PLANES), pl.ds(at, edge_rows)], edge_ref, sem.at[0]
    )
    edge.start()
    run([
        pltpu.make_async_copy(sources, source_ref, sem.at[1]),
        pltpu.make_async_copy(slots, slot_ref, sem.at[2]),
    ])
    me = me_ref[0]
    copies = []
    for ref, offset, start in ((up_ref, 1, HALF), (down_ref, -1, 0)):
        for i, pick in enumerate(needed(source_ref, slot_ref, me, offset, devices)):
            copies.append(
                pltpu.make_async_copy(
                    wave_ref.at[pick, :, pl.ds(1 + start, HALF)], ref.at[i], sem.at[3 + len(copies)]
                )
            )
    run(copies)
    edge.wait()


def item_kernel(
    devices, me_ref, sources, slots, pair_ref, order_ref, count_ref, item_ref, pass_ref, source_ref, slot_ref, sem
):
    run([
        pltpu.make_async_copy(sources, source_ref, sem.at[0]),
        pltpu.make_async_copy(slots, slot_ref, sem.at[1]),
    ])
    me = me_ref[0]

    def other(by):
        return lax.rem(me + by + devices, devices)

    for i, (by, offset) in enumerate(((-1, 2), (-1, -2), (1, -2), (1, 2))):
        pair = needed(source_ref, slot_ref, other(by), offset, devices)
        pass_ref[2 * i] = pair[0]
        pass_ref[2 * i + 1] = pair[1]
    firsts = [needed(source_ref, slot_ref, other(by), -by, devices)[0] for by in (-1, 1, -2, 2)]
    for g in range(GROUPS):
        count_ref[g] = jnp.int32(0)
    for s in range(HELD):
        for e in range(PARTS):
            slot = slot_ref[source_ref[e, me * HELD + s]]
            local, offset = slot % HELD, slot // HELD - me
            group, first = jnp.int32(0), jnp.int32(0)
            for g, by in enumerate((-1, 1, -2, 2)):
                group = jnp.where(offset == by, g + 1, group)
                first = jnp.where(offset == by, firsts[g], first)
            place = jnp.where(local == first, 0, 1)
            field = pair_ref[s, e] * ORDERS + order_ref[s, e]
            number = count_ref[group]
            item_ref[group, number] = (s * PARTS + e) + ENTRIES * (local + HELD * (place + 2 * field))
            count_ref[group] = number + 1


def pass_kernel(first, pass_ref, all_ref, one_ref, three_ref):
    for i in range(2):
        one_ref[i] = all_ref[pass_ref[first + i]]
        three_ref[i] = all_ref[pass_ref[first + 2 + i]]


def radius(shape, dim, start):
    return (start + lax.broadcasted_iota(jnp.int32, shape, dim) + 1).astype(jnp.float32) * grid_step


def field_kernel(row_ref, *out_refs):
    shape = out_refs[0].shape[1:]
    step = 16

    def tile(i, carry):
        at = pl.ds(pl.multiple_of(i * step, step), step)
        part = (step, shape[1])
        r_one = radius(part, 0, row_ref[0] + i * step)
        r_two = radius(part, 1, 0)

        def write(refs, pair, left, right):
            greater = jnp.maximum(left, right)
            value = 1.0 / greater
            ratio = jnp.minimum(left, right) / greater
            for order in range(ORDERS):
                for ref in refs:
                    ref[pair * ORDERS + order, at] = jnp.broadcast_to(value, part)
                value = value * ratio

        write(out_refs, 0, r_one, r_two)
        for p, ref in enumerate(out_refs):
            r_three = (WSTART + p + 1) * grid_step
            write([ref], 1, r_one, r_three)
            write([ref], 2, r_two, r_three)
        return carry

    lax.fori_loop(0, shape[0] // step, tile, 0)


def diagonal_kernel(row_ref, l_ref, wave_ref, edge_ref, out_ref):
    s, c = pl.program_id(0), pl.program_id(1)
    rows, columns = wave_ref.shape[3:]
    shape = (rows, columns)
    r_one = radius((rows, 1), 0, row_ref[0])
    r_two = radius((1, columns), 1, 0)

    def centrifugal(electron):
        number = l_ref[s, electron].astype(jnp.float32)
        return number * (number + 1.0)

    first = centrifugal(0) / (2.0 * r_one * r_one) - charge / r_one
    second = centrifugal(1) / (2.0 * r_two * r_two) - charge / r_two
    sign = jnp.where(c == 1, time_step, -time_step)
    lower_half = row_ref[0] == 0
    row = lax.broadcasted_iota(jnp.int32, shape, 0)
    column = lax.broadcasted_iota(jnp.int32, shape, 1)
    for p in range(PLANES):
        r_three = (WSTART + p + 1) * grid_step
        third = centrifugal(2) / (2.0 * r_three * r_three) - charge / r_three
        centre = wave_ref[0, 0, p + 1].astype(jnp.float32)
        edge = edge_ref[0, 0, p].astype(jnp.float32)
        above = jnp.where(lower_half, 0.0, edge[-1:])
        below = jnp.where(lower_half, edge[:1], 0.0)
        total = wave_ref[0, 0, p].astype(jnp.float32) + wave_ref[0, 0, p + 2].astype(jnp.float32)
        total = total + jnp.where(row == 0, above, pltpu.roll(centre, 1, 0))
        total = total + jnp.where(row == rows - 1, below, pltpu.roll(centre, rows - 1, 0))
        total = total + jnp.where(column == 0, 0.0, pltpu.roll(centre, 1, 1))
        total = total + jnp.where(column == columns - 1, 0.0, pltpu.roll(centre, columns - 1, 1))
        potential = first + (second + (third + 3.0 / (grid_step * grid_step)))
        energy = potential * centre - (0.5 / (grid_step * grid_step)) * total
        out_ref[0, 0, p] = (sign * energy).astype(out_ref.dtype)


def add_items(group, selected, p, count_ref, item_ref, weight_ref, field_ref, source_ref, total):
    rows = total.shape[2]
    step = 16

    def one(n, carry):
        code = item_ref[group, n]
        entry, rest = code % ENTRIES, code // ENTRIES
        s, e = entry // PARTS, entry % PARTS
        local, rest = rest % HELD, rest // HELD
        place, field = rest % 2, rest // 2
        place = place if selected else local
        weight = weight_ref[s, e]
        for i in range(rows // step):
            at = pl.ds(i * step, step)
            factor = weight * field_ref[field, at]
            for c in range(2):
                total[s, c, at] += factor * source_ref[place, c, p, at].astype(jnp.float32)
        return carry

    lax.fori_loop(0, count_ref[group], one, 0)


def own_kernel(count_ref, item_ref, weight_ref, wave_ref, up_all, down_all, *refs):
    fields, totals, own, sem = refs[:PLANES], refs[PLANES : 2 * PLANES], refs[-2], refs[-1]
    copy = pltpu.make_async_copy(wave_ref.at[:, :, pl.ds(1, PLANES)], own, sem)
    copy.start()
    for total in totals:
        total[...] = jnp.zeros_like(total)
    copy.wait()
    for p in range(PLANES):
        common = count_ref, item_ref, weight_ref, fields[p]
        add_items(0, False, p, *common, own, totals[p])
        group, ref = (1, up_all) if p < HALF else (2, down_all)
        add_items(group, False, p % HALF, *common, ref, totals[p])


def near_kernel(count_ref, item_ref, weight_ref, up_two, down_two, *refs):
    fields, totals = refs[:PLANES], refs[-PLANES:]
    for p in range(PLANES):
        group, ref = (2, down_two) if p < HALF else (1, up_two)
        add_items(group, True, p % HALF, count_ref, item_ref, weight_ref, fields[p], ref, totals[p])


def last_kernel(count_ref, item_ref, weight_ref, up_one, down_three, down_one, up_three, *refs):
    fields, totals = refs[:PLANES], refs[-2 - PLANES : -2]
    out_ref, (staged, sem) = refs[-3 - PLANES], refs[-2:]
    copies = []
    for p, total in enumerate(totals):
        common = count_ref, item_ref, weight_ref, fields[p]
        for group, ref in ((3, up_one), (4, down_three)) if p < HALF else ((4, down_one), (3, up_three)):
            add_items(group, True, p % HALF, *common, ref, total)
        for s in range(HELD):
            staged[p, s, 0] = total[s, 1].astype(staged.dtype)
            staged[p, s, 1] = (-total[s, 0]).astype(staged.dtype)
            copies.append(
                pltpu.make_async_copy(staged.at[p, s], out_ref.at[s, :, p], sem.at[p * HELD + s])
            )
            copies[-1].start()
    for copy in copies:
        copy.wait()


ANY = pl.BlockSpec(memory_space=pl.ANY)
HBM = pl.BlockSpec(memory_space=pltpu.HBM)
VMEM = pl.BlockSpec(memory_space=pltpu.VMEM)
SMEM = pl.BlockSpec(memory_space=pltpu.SMEM)


def params(mib):
    return pltpu.CompilerParams(vmem_limit_bytes=mib << 20)


def cost(micros):
    return pl.CostEstimate(flops=0, bytes_accessed=micros * 3_000_000, transcendentals=0)


def behind(value, *others):
    return lax.optimization_barrier((value, others))[0]


def shards(wave, l_values, couple_source, couple_pair, couple_order, couple_weight, channel_slot):
    devices = lax.axis_size("chan")
    rows, columns = wave.shape[3:]
    me = lax.axis_index("chan").astype(jnp.int32).reshape(1)
    core = lax.axis_index("radial").astype(jnp.int32)
    row_start = (core * rows).reshape(1)
    bf16 = wave.dtype

    def array(*lead, dtype=bf16):
        return jax.ShapeDtypeStruct((*lead, rows, columns), dtype)

    sources = couple_source.T
    index_scratch = [pltpu.SMEM(sources.shape, jnp.int32), pltpu.SMEM(channel_slot.shape, jnp.int32)]

    def dma(number):
        return pltpu.SemaphoreType.DMA((number,))

    def shift(array, by):
        return lax.ppermute(array, "chan", [(i, (i + by) % devices) for i in range(devices)])

    up_all, down_all = pl.pallas_call(
        head_kernel,
        out_shape=[array(HELD, 2, HALF)] * 2,
        in_specs=[HBM],
        out_specs=[ANY] * 2,
        scratch_shapes=[pltpu.VMEM((HELD, 2, HALF, rows, columns), bf16)] * 2 + [dma(2 * HELD)] * 2,
        compiler_params=params(60),
        cost_estimate=cost(2),
        name="head_kernel",
    )(wave)
    wave = behind(wave, up_all)
    up_all, down_all = shift(up_all, 1), shift(down_all, -1)
    up_two, down_two, edge = pl.pallas_call(
        functools.partial(select_kernel, devices, EDGE),
        out_shape=[*[array(2, 2, HALF)] * 2, jax.ShapeDtypeStruct((HELD, 2, PLANES, EDGE, columns), bf16)],
        in_specs=[SMEM, SMEM, HBM, HBM, HBM],
        out_specs=[VMEM] * 3,
        scratch_shapes=[*index_scratch, dma(7)],
        compiler_params=params(60),
        cost_estimate=cost(3),
        name="select_kernel",
    )(me, core.reshape(1), sources, channel_slot, wave)
    me_late, start_late = behind((me, row_start), up_two)
    up_two = shift(up_two, 1)
    down_two = shift(down_two, -1)
    edge = lax.ppermute(edge, "radial", [(0, 1), (1, 0)])

    count, item, passed = pl.pallas_call(
        functools.partial(item_kernel, devices),
        out_shape=(
            jax.ShapeDtypeStruct((GROUPS,), jnp.int32),
            jax.ShapeDtypeStruct((GROUPS, ENTRIES), jnp.int32),
            jax.ShapeDtypeStruct((8,), jnp.int32),
        ),
        in_specs=[SMEM, HBM, HBM, SMEM, SMEM],
        out_specs=(SMEM,) * 3,
        scratch_shapes=[*index_scratch, dma(2)],
        compiler_params=params(4),
        cost_estimate=cost(6),
        name="item_kernel",
    )(me_late, sources, channel_slot, couple_pair, couple_order)

    fields = pl.pallas_call(
        field_kernel,
        out_shape=[array(3 * ORDERS, dtype=jnp.float32)] * PLANES,
        in_specs=[SMEM],
        out_specs=[VMEM] * PLANES,
        compiler_params=params(16),
        cost_estimate=cost(2),
        name="field_kernel",
    )(behind(start_late, count))

    diag_step = pl.pallas_call(
        diagonal_kernel,
        grid=(HELD, 2),
        out_shape=array(HELD, 2, PLANES),
        in_specs=[
            SMEM,
            SMEM,
            pl.BlockSpec((1, 1, PLANES + 2, rows, columns), lambda s, c: (s, c, 0, 0, 0)),
            pl.BlockSpec((1, 1, PLANES, EDGE, columns), lambda s, c: (s, c, 0, 0, 0)),
        ],
        out_specs=pl.BlockSpec((1, 1, PLANES, rows, columns), lambda s, c: (s, 1 - c, 0, 0, 0)),
        compiler_params=params(10),
        cost_estimate=cost(7),
        name="diagonal_kernel",
    )(behind(start_late, fields), l_values, wave, edge)

    def passing(first, source, *others):
        return pl.pallas_call(
            functools.partial(pass_kernel, first),
            out_shape=[array(2, 2, HALF)] * 2,
            in_specs=[SMEM, VMEM],
            out_specs=[VMEM] * 2,
            compiler_params=params(8),
            cost_estimate=cost(1),
            name="pass_kernel",
        )(behind(passed, *others), source)

    up_one, down_three = passing(0, up_all, diag_step)
    down_one, up_three = passing(4, down_all, up_one)
    weights = behind(couple_weight, up_three)
    moved = [shift(v, by) for v, by in ((up_one, 1), (down_three, -3), (down_one, -1), (up_three, 3))]
    tables = [count, item, weights]
    totals = pl.pallas_call(
        own_kernel,
        out_shape=[array(HELD, 2, dtype=jnp.float32)] * PLANES,
        in_specs=[SMEM] * 3 + [HBM] + [VMEM] * (2 + PLANES),
        out_specs=[VMEM] * PLANES,
        scratch_shapes=[pltpu.VMEM((HELD, 2, PLANES, rows, columns), bf16), pltpu.SemaphoreType.DMA(())],
        compiler_params=params(8),
        cost_estimate=cost(9),
        name="own_kernel",
    )(*tables, wave, up_all, down_all, *fields)
    totals = pl.pallas_call(
        near_kernel,
        out_shape=[array(HELD, 2, dtype=jnp.float32)] * PLANES,
        in_specs=[SMEM] * 3 + [VMEM] * (2 + 2 * PLANES),
        out_specs=[VMEM] * PLANES,
        input_output_aliases={5 + PLANES + p: p for p in range(PLANES)},
        compiler_params=params(8),
        cost_estimate=cost(4),
        name="near_kernel",
    )(*tables, up_two, down_two, *fields, *totals)

    inputs = [*tables, *moved, *fields, *totals]
    coupling, *_ = pl.pallas_call(
        last_kernel,
        out_shape=[array(HELD, 2, PLANES)] + [array(HELD, 2, dtype=jnp.float32)] * PLANES,
        in_specs=[SMEM] * 3 + [VMEM] * (len(inputs) - 3),
        out_specs=[ANY] + [VMEM] * PLANES,
        scratch_shapes=[pltpu.VMEM((PLANES, HELD, 2, rows, columns), bf16), dma(PLANES * HELD)],
        input_output_aliases={len(inputs) - PLANES + p: 1 + p for p in range(PLANES)},
        compiler_params=params(16),
        cost_estimate=cost(3),
        name="last_kernel",
    )(*inputs)
    return diag_step, coupling


def solution(mesh):
    placed = (
        P("chan", None, None, "radial", None),
        P("chan", None),
        P(),
        P("chan", None),
        P("chan", None),
        P("chan", None),
        P(),
    )
    return jax.shard_map(
        shards,
        mesh=mesh,
        in_specs=placed,
        out_specs=(P("chan", None, None, "radial", None), P("chan", None, None, "radial", None)),
        check_vma=False,
    )
```

time: 127 us -> 104 us (0.82)
  the two profiles are of different devices: /device:TPU:0 before, /device:TPU:254 now
where the time goes in v1:
time: 104 us; the launch traced here: 105 us
  waiting for transfers between devices  48.4 us (47%)
  Pallas kernels  35.5 us (34%)
  starting transfers between devices  15.2 us (15%)
  local copies, waits for them, and re-layouts  5.07 us (5%)
    ppermute x8, waiting for transfers between devices, shift(): lax.ppermute(array, 'chan', [(i, (i + by) % devices) for i in range(devic...  48.4 us
    ppermute x8, starting transfers between devices, shift(): lax.ppermute(array, 'chan', [(i, (i + by) % devices) for i in range(devic...  15.2 us
    pallas_call x1, Pallas kernels, shards(): pl.pallas_call(diagonal_kernel, grid=(HELD, 2), out_shape=array(HELD, 2,...  7.13 us
    pallas_call x1, Pallas kernels, shards(): pl.pallas_call(own_kernel, out_shape=[array(HELD, 2, dtype=jnp.float32)]...  6.74 us
    pallas_call x1, Pallas kernels, shards(): pl.pallas_call(last_kernel, out_shape=[array(HELD, 2, PLANES)] + [array(H...  6.03 us
    unnamed x16, local copies, waits for them, and re-layouts  5.07 us
    pallas_call x1, Pallas kernels, shards(): pl.pallas_call(functools.partial(item_kernel, devices), out_shape=(jax.Sh...  4.52 us
    pallas_call x1, Pallas kernels, shards(): pl.pallas_call(functools.partial(select_kernel, devices, EDGE), out_shape...  4.07 us
  transfers between devices with their start and end apart: 9, of which 7 were waited for; matrix products, arithmetic and copies ran while one was open for 0% of the time, Pallas kernels for 25%

profile of v1, /device:TPU:254, one launch (start us, length us, event | category | flops | bytes accessed | tf_op | source)
XLA Modules:
  0.0 104.8 jit_solution(9749125171400653942)
XLA Ops:
  0.6 2.8 %head_kernel.1 = (bf16[4,2,2,128,384]{4,3,2,1,0:T(8,128)(2,1)}, bf16[4,2,2,128,384]{4,3,2,1,0:T(8,128)(2,1)}) custom-call(bf16[4,2,6,128,384]{4,3,2,1,0:T(8,128)(2,1)} %wave_ref.4), custom_call_target="tpu_custom_call" | custom-call | bytes 6000000 | tf_op jit(solution)/shard_map/head_kernel/pallas_call | solution.py:316
  3.4 0.1 collective-permute-start.1
  3.5 2.0 %collective-permute-start.2 = (bf16[4,2,2,128,384]{4,3,2,1,0:T(8,128)(2,1)}, bf16[4,2,2,128,384]{4,3,2,1,0:T(8,128)(2,1)S(1)}, u32[]{:S(2)}, u32[]{:S(2)}) collective-permute-start(bf16[4,2,2,128,384]{4,3,2,1,0:T(8,128)(2,1)} %get-tuple-element.53), channel_id=1, source_target_pairs={{0,254},{2,0},{4,2},{6,4},{8,6},{10,8},{12,10},{14,12},{16,14},{18... | collective-permute-start | bytes 4718600 | tf_op jit(solution)/shard_map/ppermute | solution.py:314
  5.5 4.1 %select_kernel.1 = (bf16[2,2,2,128,384]{4,3,2,1,0:T(8,128)(2,1)}, bf16[2,2,2,128,384]{4,3,2,1,0:T(8,128)(2,1)}, bf16[4,2,4,16,384]{4,3,2,1,0:T(8,128)(2,1)}) custom-call(s32[1]{0:T(128)} %bitcast.me_ref, s32[1]{0:T(128)} %bitcast.2.core_ref, s32[8,512]{1,0:T(8,128)} %bitcast.4, s32[512]{0:T(512)} %slots.3, bf16[4,2,6,128,384]{4,3,2,1,0:T(8,128)(2,1)} %wave_ref.4), custom_call_target="tpu_custom_call" | custom-call | bytes 9000000 | tf_op jit(solution)/shard_map/select_kernel/pallas_call | solution.py:328
  9.6 0.8 collective-permute-start.8
  10.4 0.0 collective-permute-start
  10.4 6.7 %collective-permute-start.7 = (bf16[2,2,2,128,384]{4,3,2,1,0:T(8,128)(2,1)}, bf16[2,2,2,128,384]{4,3,2,1,0:T(8,128)(2,1)}, u32[]{:S(2)}, u32[]{:S(2)}) collective-permute-start(bf16[2,2,2,128,384]{4,3,2,1,0:T(8,128)(2,1)} %get-tuple-element.37), channel_id=1, source_target_pairs={{0,2},{2,4},{4,6},{6,8},{8,10},{10,12},{12,14},{14,16},{16,18},{18... | collective-permute-start | bytes 2359304 | tf_op jit(solution)/shard_map/ppermute | solution.py:314
  17.2 0.7 copy-done.4
  17.8 0.7 copy-done.6
  18.5 0.7 copy-done.7
  19.2 4.5 %item_kernel.1 = (s32[5]{0:T(128)S(1)}, s32[5,32]{1,0:T(8,128)S(1)}, s32[8]{0:T(128)S(1)}) custom-call(s32[1]{0:T(128)} %bitcast.me_ref, s32[8,512]{1,0:T(8,128)S(1)} %bitcast.5, s32[512]{0:T(512)S(1)} %copy-done.4, s32[4,8]{1,0:T(4,128)S(1)} %copy-done.6, s32[4,8]{1,0:T(4,128)S(1)} %copy-done.7), custom_call_target="tpu_custom_call" | custom-call | bytes 18000000 | tf_op jit(solution)/shard_map/item_kernel/pallas_call | solution.py:343
  23.7 0.7 field_kernel.1
  24.5 0.0 collective-permute-done.edge_ref
  24.5 0.0 copy-start
  24.5 2.3 %copy-done = bf16[4,2,6,128,384]{4,3,2,1,0:T(8,128)(2,1)S(1)} copy-done((bf16[4,2,6,128,384]{4,3,2,1,0:T(8,128)(2,1)S(1)}, bf16[4,2,6,128,384]{4,3,2,1,0:T(8,128)(2,1)}, u32[]{:S(2)}) %copy-start) | copy-done | bytes 4718616
  26.8 0.7 copy-done.5
  27.5 7.1 %diagonal_kernel.1 = bf16[4,2,4,128,384]{4,3,2,1,0:T(8,128)(2,1)} custom-call(s32[1]{0:T(128)} %bitcast.1.row_ref, s32[4,3]{1,0:T(4,128)S(1)} %copy-done.5, bf16[4,2,6,128,384]{4,3,2,1,0:T(8,128)(2,1)S(1)} %copy-done, bf16[4,2,4,16,384]{4,3,2,1,0:T(8,128)(2,1)S(1)} %collective-permute-done.edge_ref), custom_call_target="tpu_custom_call" | custom-call | bytes 21000000 | tf_op jit(solution)/shard_map/diagonal_kernel/pallas_call | solution.py:368
  34.6 6.3 %collective-permute-done.1.all_ref.up_all = bf16[4,2,2,128,384]{4,3,2,1,0:T(8,128)(2,1)S(1)} collective-permute-done((bf16[4,2,2,128,384]{4,3,2,1,0:T(8,128)(2,1)}, bf16[4,2,2,128,384]{4,3,2,1,0:T(8,128)(2,1)S(1)}, u32[]{:S(2)}, u32[]{:S(2)}) %collective-permute-start.1) | collective-permute-done | bytes 1572896 | tf_op jit(solution)/shard_map/ppermute | solution.py:314
  41.0 0.7 pass_kernel.2
  41.7 5.5 %collective-permute-start.3 = (bf16[2,2,2,128,384]{4,3,2,1,0:T(8,128)(2,1)S(1)}, bf16[2,2,2,128,384]{4,3,2,1,0:T(8,128)(2,1)S(1)}, u32[]{:S(2)}, u32[]{:S(2)}) collective-permute-start(bf16[2,2,2,128,384]{4,3,2,1,0:T(8,128)(2,1)S(1)} %get-tuple-element.51), channel_id=1, source_target_pairs={{0,2},{2,4},{4,6},{6,8},{8,10},{10,12},{12,14},{14,16},{16,18},{18... | collective-permute-start | bytes 2359304 | tf_op jit(solution)/shard_map/ppermute | solution.py:314
  47.2 0.7 pass_kernel.3
  47.9 0.1 collective-permute-start.5
  47.9 15.5 %collective-permute-done.8.down_two = bf16[2,2,2,128,384]{4,3,2,1,0:T(8,128)(2,1)} collective-permute-done((bf16[2,2,2,128,384]{4,3,2,1,0:T(8,128)(2,1)}, bf16[2,2,2,128,384]{4,3,2,1,0:T(8,128)(2,1)}, u32[]{:S(2)}, u32[]{:S(2)}) %collective-permute-start.8) | collective-permute-done | bytes 786464 | tf_op jit(solution)/shard_map/ppermute | solution.py:314
  63.5 0.0 collective-permute-start.6
  63.5 6.7 %own_kernel.1 = (f32[4,2,128,384]{3,2,1,0:T(8,128)S(1)}, f32[4,2,128,384]{3,2,1,0:T(8,128)S(1)}, f32[4,2,128,384]{3,2,1,0:T(8,128)S(1)}, f32[4,2,128,384]{3,2,1,0:T(8,128)S(1)}) custom-call(s32[5]{0:T(128)S(1)} %get-tuple-element.40.count_ref, s32[5,32]{1,0:T(8,128)S(1)} %get-tuple-element.48.item_ref, f32[4,8]{1,0:T(4,128)S(1)} %copy-done.3, ...), custom_call_target="tpu_custom_call" | custom-call | bytes 27000000 | tf_op jit(solution)/shard_map/own_kernel/pallas_call | solution.py:400
  70.2 4.6 %collective-permute-done.7.up_two = bf16[2,2,2,128,384]{4,3,2,1,0:T(8,128)(2,1)} collective-permute-done((bf16[2,2,2,128,384]{4,3,2,1,0:T(8,128)(2,1)}, bf16[2,2,2,128,384]{4,3,2,1,0:T(8,128)(2,1)}, u32[]{:S(2)}, u32[]{:S(2)}) %collective-permute-start.7) | collective-permute-done | bytes 786464 | tf_op jit(solution)/shard_map/ppermute | solution.py:314
  74.8 2.1 %near_kernel.1 = (f32[4,2,128,384]{3,2,1,0:T(8,128)S(1)}, f32[4,2,128,384]{3,2,1,0:T(8,128)S(1)}, f32[4,2,128,384]{3,2,1,0:T(8,128)S(1)}, f32[4,2,128,384]{3,2,1,0:T(8,128)S(1)}) custom-call(s32[5]{0:T(128)S(1)} %get-tuple-element.40.count_ref, ...), custom_call_target="tpu_custom_call", output_to_operand_aliasing={{0}: (9, {}), {1}: (10, {}), {2}: (11, {}), {3}: (12, {})} | custom-call | bytes 12000000 | tf_op jit(solution)/shard_map/near_kernel/pallas_call | solution.py:410
  76.9 12.2 %collective-permute-done.4.down_three = bf16[2,2,2,128,384]{4,3,2,1,0:T(8,128)(2,1)S(1)} collective-permute-done((bf16[2,2,2,128,384]{4,3,2,1,0:T(8,128)(2,1)S(1)}, bf16[2,2,2,128,384]{4,3,2,1,0:T(8,128)(2,1)S(1)}, u32[]{:S(2)}, u32[]{:S(2)}) %collective-permute-start.4) | collective-permute-done | bytes 786464 | tf_op jit(solution)/shard_map/ppermute | solution.py:314
  89.0 1.4 %collective-permute-done.3.up_one = bf16[2,2,2,128,384]{4,3,2,1,0:T(8,128)(2,1)S(1)} collective-permute-done((bf16[2,2,2,128,384]{4,3,2,1,0:T(8,128)(2,1)S(1)}, bf16[2,2,2,128,384]{4,3,2,1,0:T(8,128)(2,1)S(1)}, u32[]{:S(2)}, u32[]{:S(2)}) %collective-permute-start.3) | collective-permute-done | bytes 786464 | tf_op jit(solution)/shard_map/ppermute | solution.py:314
  90.4 5.7 %collective-permute-done.5.down_one = bf16[2,2,2,128,384]{4,3,2,1,0:T(8,128)(2,1)S(1)} collective-permute-done((bf16[2,2,2,128,384]{4,3,2,1,0:T(8,128)(2,1)S(1)}, bf16[2,2,2,128,384]{4,3,2,1,0:T(8,128)(2,1)S(1)}, u32[]{:S(2)}, u32[]{:S(2)}) %collective-permute-start.5) | collective-permute-done | bytes 786464 | tf_op jit(solution)/shard_map/ppermute | solution.py:314
  96.1 2.7 %collective-permute-done.6.up_three = bf16[2,2,2,128,384]{4,3,2,1,0:T(8,128)(2,1)S(1)} collective-permute-done((bf16[2,2,2,128,384]{4,3,2,1,0:T(8,128)(2,1)S(1)}, bf16[2,2,2,128,384]{4,3,2,1,0:T(8,128)(2,1)S(1)}, u32[]{:S(2)}, u32[]{:S(2)}) %collective-permute-start.6) | collective-permute-done | bytes 786464 | tf_op jit(solution)/shard_map/ppermute | solution.py:314
  98.8 6.0 %last_kernel.1 = (bf16[4,2,4,128,384]{4,3,2,1,0:T(8,128)(2,1)}, f32[4,2,128,384]{3,2,1,0:T(8,128)S(1)}, f32[4,2,128,384]{3,2,1,0:T(8,128)S(1)}, f32[4,2,128,384]{3,2,1,0:T(8,128)S(1)}, f32[4,2,128,384]{3,2,1,0:T(8,128)S(1)}) custom-call(s32[5]{0:T(128)S(1)} %get-tuple-element.40.count_ref, ...), custom_call_target="tpu_custom_call", output_to_operand_aliasing={{1}: (11, {}), {2}: (12, {}), {3}: (13, {}), {4}: (14, {})} | custom-call | bytes 9000000 | tf_op jit(solution)/shard_map/last_kernel/pallas_call | solution.py:422
  (12 shorter events, 0.0 us)
Async XLA Ops:
  3.4 37.6 %collective-permute-start.1 = (bf16[4,2,2,128,384]{4,3,2,1,0:T(8,128)(2,1)}, bf16[4,2,2,128,384]{4,3,2,1,0:T(8,128)(2,1)S(1)}, u32[]{:S(2)}, u32[]{:S(2)}) collective-permute-start(bf16[4,2,2,128,384]{4,3,2,1,0:T(8,128)(2,1)} %get-tuple-element.35), channel_id=1, source_target_pairs={{0,2},{2,4},{4,6},{6,8},{8,10},{10,12},{12,14},{14,16},{16,18},{18... | collective-permute-start | bytes 4718600 | tf_op jit(solution)/shard_map/ppermute | solution.py:314
  3.5 43.6 %collective-permute-start.2 = (bf16[4,2,2,128,384]{4,3,2,1,0:T(8,128)(2,1)}, bf16[4,2,2,128,384]{4,3,2,1,0:T(8,128)(2,1)S(1)}, u32[]{:S(2)}, u32[]{:S(2)}) collective-permute-start(bf16[4,2,2,128,384]{4,3,2,1,0:T(8,128)(2,1)} %get-tuple-element.53), channel_id=1, source_target_pairs={{0,254},{2,0},{4,2},{6,4},{8,6},{10,8},{12,10},{14,12},{16,14},{18... | collective-permute-start | bytes 4718600 | tf_op jit(solution)/shard_map/ppermute | solution.py:314
  5.5 11.6 %copy-start.2 = (s32[512,8]{0,1:T(8,128)S(1)}, s32[512,8]{0,1:T(8,128)}, u32[]{:S(2)}) copy-start(s32[512,8]{0,1:T(8,128)} %param.9) | copy-start | bytes 49156
  9.6 53.9 %collective-permute-start.8 = (bf16[2,2,2,128,384]{4,3,2,1,0:T(8,128)(2,1)}, bf16[2,2,2,128,384]{4,3,2,1,0:T(8,128)(2,1)}, u32[]{:S(2)}, u32[]{:S(2)}) collective-permute-start(bf16[2,2,2,128,384]{4,3,2,1,0:T(8,128)(2,1)} %get-tuple-element.58), channel_id=1, source_target_pairs={{0,254},{2,0},{4,2},{6,4},{8,6},{10,8},{12,10},{14,12},{16,14},{18... | collective-permute-start | bytes 2359304 | tf_op jit(solution)/shard_map/ppermute | solution.py:314
  10.4 14.0 %collective-permute-start = (bf16[4,2,4,16,384]{4,3,2,1,0:T(8,128)(2,1)}, bf16[4,2,4,16,384]{4,3,2,1,0:T(8,128)(2,1)S(1)}, u32[]{:S(2)}, u32[]{:S(2)}) collective-permute-start(bf16[4,2,4,16,384]{4,3,2,1,0:T(8,128)(2,1)} %get-tuple-element.47), channel_id=1, source_target_pairs={{0,1},{1,0},{2,3},{3,2},{4,5},{5,4},{6,7},{7,6},{8,9},{9,8},{10,11... | collective-permute-start | bytes 1179656 | tf_op jit(solution)/shard_map/ppermute | solution.py:341
  10.4 64.4 %collective-permute-start.7 = (bf16[2,2,2,128,384]{4,3,2,1,0:T(8,128)(2,1)}, bf16[2,2,2,128,384]{4,3,2,1,0:T(8,128)(2,1)}, u32[]{:S(2)}, u32[]{:S(2)}) collective-permute-start(bf16[2,2,2,128,384]{4,3,2,1,0:T(8,128)(2,1)} %get-tuple-element.37), channel_id=1, source_target_pairs={{0,2},{2,4},{4,6},{6,8},{8,10},{10,12},{12,14},{14,16},{16,18},{18... | collective-permute-start | bytes 2359304 | tf_op jit(solution)/shard_map/ppermute | solution.py:314
  17.2 0.7 copy-start.4
  17.8 0.7 copy-start.6
  18.5 0.7 copy-start.7
  24.5 2.3 %copy-start = (bf16[4,2,6,128,384]{4,3,2,1,0:T(8,128)(2,1)S(1)}, bf16[4,2,6,128,384]{4,3,2,1,0:T(8,128)(2,1)}, u32[]{:S(2)}) copy-start(bf16[4,2,6,128,384]{4,3,2,1,0:T(8,128)(2,1)} %wave_ref.4) | copy-start | bytes 14155780
  26.8 0.7 copy-start.5
  27.5 36.0 %copy-start.1 = (bf16[4,2,6,128,384]{4,3,2,1,0:T(8,128)(2,1)S(1)}, bf16[4,2,6,128,384]{4,3,2,1,0:T(8,128)(2,1)}, u32[]{:S(2)}) copy-start(bf16[4,2,6,128,384]{4,3,2,1,0:T(8,128)(2,1)} %wave_ref.4) | copy-start | bytes 14155780
  34.6 28.8 %copy-start.3 = (f32[4,8]{1,0:T(4,128)S(1)}, f32[4,8]{1,0:T(4,128)}, u32[]{:S(2)}) copy-start(f32[4,8]{1,0:T(4,128)} %weight_ref.2) | copy-start | bytes 388
  41.7 48.7 %collective-permute-start.3 = (bf16[2,2,2,128,384]{4,3,2,1,0:T(8,128)(2,1)S(1)}, bf16[2,2,2,128,384]{4,3,2,1,0:T(8,128)(2,1)S(1)}, u32[]{:S(2)}, u32[]{:S(2)}) collective-permute-start(bf16[2,2,2,128,384]{4,3,2,1,0:T(8,128)(2,1)S(1)} %get-tuple-element.51), channel_id=1, source_target_pairs={{0,2},{2,4},{4,6},{6,8},{8,10},{10,12},{12,14},{14,16},{16,18},{18... | collective-permute-start | bytes 2359304 | tf_op jit(solution)/shard_map/ppermute | solution.py:314
  47.2 41.9 %collective-permute-start.4 = (bf16[2,2,2,128,384]{4,3,2,1,0:T(8,128)(2,1)S(1)}, bf16[2,2,2,128,384]{4,3,2,1,0:T(8,128)(2,1)S(1)}, u32[]{:S(2)}, u32[]{:S(2)}) collective-permute-start(bf16[2,2,2,128,384]{4,3,2,1,0:T(8,128)(2,1)S(1)} %get-tuple-element.56), channel_id=1, source_target_pairs={{0,250},{2,252},{4,254},{6,0},{8,2},{10,4},{12,6},{14,8},{16,10},{... | collective-permute-start | bytes 2359304 | tf_op jit(solution)/shard_map/ppermute | solution.py:314
  47.9 48.2 %collective-permute-start.5 = (bf16[2,2,2,128,384]{4,3,2,1,0:T(8,128)(2,1)S(1)}, bf16[2,2,2,128,384]{4,3,2,1,0:T(8,128)(2,1)S(1)}, u32[]{:S(2)}, u32[]{:S(2)}) collective-permute-start(bf16[2,2,2,128,384]{4,3,2,1,0:T(8,128)(2,1)S(1)} %get-tuple-element.57), channel_id=1, source_target_pairs={{0,254},{2,0},{4,2},{6,4},{8,6},{10,8},{12,10},{14,12},{16,14},{18... | collective-permute-start | bytes 2359304 | tf_op jit(solution)/shard_map/ppermute | solution.py:314
  63.5 35.3 %collective-permute-start.6 = (bf16[2,2,2,128,384]{4,3,2,1,0:T(8,128)(2,1)S(1)}, bf16[2,2,2,128,384]{4,3,2,1,0:T(8,128)(2,1)S(1)}, u32[]{:S(2)}, u32[]{:S(2)}) collective-permute-start(bf16[2,2,2,128,384]{4,3,2,1,0:T(8,128)(2,1)S(1)} %get-tuple-element.54), channel_id=1, source_target_pairs={{0,6},{2,8},{4,10},{6,12},{8,14},{10,16},{12,18},{14,20},{16,22},{... | collective-permute-start | bytes 2359304 | tf_op jit(solution)/shard_map/ppermute | solution.py:314

commit v2 on v1

--- a/solution.py
+++ b/solution.py
@@ -256,19 +256,24 @@
         add_items(group, True, p % HALF, count_ref, item_ref, weight_ref, fields[p], ref, totals[p])
 
 
-def last_kernel(count_ref, item_ref, weight_ref, up_one, down_three, down_one, up_three, *refs):
-    fields, totals = refs[:PLANES], refs[-2 - PLANES : -2]
-    out_ref, (staged, sem) = refs[-3 - PLANES], refs[-2:]
+def far_kernel(count_ref, item_ref, weight_ref, down_one, *refs):
+    fields, totals = refs[:HALF], refs[-HALF:]
+    for p in range(HALF):
+        add_items(4, True, p, count_ref, item_ref, weight_ref, fields[p], down_one, totals[p])
+
+
+def last_kernel(start, groups, count_ref, item_ref, weight_ref, *refs):
+    fars, fields = refs[: len(groups)], refs[len(groups) : len(groups) + HALF]
+    totals, out_ref, (staged, sem) = refs[-2 - HALF : -2], refs[-3 - HALF], refs[-2:]
     copies = []
     for p, total in enumerate(totals):
-        common = count_ref, item_ref, weight_ref, fields[p]
-        for group, ref in ((3, up_one), (4, down_three)) if p < HALF else ((4, down_one), (3, up_three)):
-            add_items(group, True, p % HALF, *common, ref, total)
+        for group, ref in zip(groups, fars):
+            add_items(group, True, p, count_ref, item_ref, weight_ref, fields[p], ref, total)
         for s in range(HELD):
             staged[p, s, 0] = total[s, 1].astype(staged.dtype)
             staged[p, s, 1] = (-total[s, 0]).astype(staged.dtype)
             copies.append(
-                pltpu.make_async_copy(staged.at[p, s], out_ref.at[s, :, p], sem.at[p * HELD + s])
+                pltpu.make_async_copy(staged.at[p, s], out_ref.at[s, :, start + p], sem.at[p * HELD + s])
             )
             copies[-1].start()
     for copy in copies:
@@ -312,6 +317,14 @@
 
     def shift(array, by):
         return lax.ppermute(array, "chan", [(i, (i + by) % devices) for i in range(devices)])
+
+    def onward(array, source, by):
+        pairs = []
+        for i in range(devices):
+            origin, target = (i + source) % devices, (i + by) % devices
+            if abs(origin - target) == 2:
+                pairs.append((i, target))
+        return lax.ppermute(array, "chan", pairs)
 
     up_all, down_all = pl.pallas_call(
         head_kernel,
@@ -395,7 +408,10 @@
     up_one, down_three = passing(0, up_all, diag_step)
     down_one, up_three = passing(4, down_all, up_one)
     weights = behind(couple_weight, up_three)
-    moved = [shift(v, by) for v, by in ((up_one, 1), (down_three, -3), (down_one, -1), (up_three, 3))]
+    moved = [
+        onward(v, *where)
+        for v, where in ((up_one, (-1, 1)), (down_three, (-1, -3)), (down_one, (1, -1)), (up_three, (1, 3)))
+    ]
     tables = [count, item, weights]
     totals = pl.pallas_call(
         own_kernel,
@@ -418,18 +434,38 @@
         name="near_kernel",
     )(*tables, up_two, down_two, *fields, *totals)
 
-    inputs = [*tables, *moved, *fields, *totals]
-    coupling, *_ = pl.pallas_call(
-        last_kernel,
-        out_shape=[array(HELD, 2, PLANES)] + [array(HELD, 2, dtype=jnp.float32)] * PLANES,
+    up_one, down_three, down_one, up_three = moved
+    inputs = [*tables, down_one, *fields[HALF:], *totals[HALF:]]
+    late = pl.pallas_call(
+        far_kernel,
+        out_shape=[array(HELD, 2, dtype=jnp.float32)] * HALF,
         in_specs=[SMEM] * 3 + [VMEM] * (len(inputs) - 3),
-        out_specs=[ANY] + [VMEM] * PLANES,
-        scratch_shapes=[pltpu.VMEM((PLANES, HELD, 2, rows, columns), bf16), dma(PLANES * HELD)],
-        input_output_aliases={len(inputs) - PLANES + p: 1 + p for p in range(PLANES)},
-        compiler_params=params(16),
-        cost_estimate=cost(3),
-        name="last_kernel",
+        out_specs=[VMEM] * HALF,
+        input_output_aliases={len(inputs) - HALF + p: p for p in range(HALF)},
+        compiler_params=params(8),
+        cost_estimate=cost(1),
+        name="far_kernel",
     )(*inputs)
+
+    def last(start, groups, fars, totals, *coupling):
+        inputs = [*tables, *fars, *fields[start : start + HALF], *totals, *coupling]
+        first = len(inputs) - len(coupling) - HALF
+        aliases = {first + p: 1 + p for p in range(HALF)} | {first + HALF: 0 for _ in coupling}
+        return pl.pallas_call(
+            functools.partial(last_kernel, start, groups),
+            out_shape=[array(HELD, 2, PLANES)] + [array(HELD, 2, dtype=jnp.float32)] * HALF,
+            in_specs=[SMEM] * 3 + [VMEM] * (first + HALF - 3) + [ANY] * len(coupling),
+            out_specs=[ANY] + [VMEM] * HALF,
+            scratch_shapes=[pltpu.VMEM((HALF, HELD, 2, rows, columns), bf16), dma(HALF * HELD)],
+            input_output_aliases=aliases,
+            compiler_params=params(12),
+            cost_estimate=cost(2),
+            name="last_kernel",
+        )(*inputs)[0]
+
+    soon = behind(totals[:HALF], late)
+    coupling = last(0, (3, 4), (up_one, down_three), soon)
+    coupling = last(HALF, (3,), (up_three,), late, coupling)
     return diag_step, coupling
 
 

time: 104 us -> 103 us (level)
  the two profiles are of different devices: /device:TPU:254 before, /device:TPU:7 now
where the time goes in v2:
time: 103 us
  Pallas kernels  36.9 us (36%)
  waiting for transfers between devices  36.3 us (35%)
  starting transfers between devices  23.8 us (23%)
  local copies, waits for them, and re-layouts  5.07 us (5%)
    ppermute x4, waiting for transfers between devices, onward(): return lax.ppermute(array, 'chan', pairs)  22.5 us
    ppermute x4, waiting for transfers between devices, shift(): lax.ppermute(array, 'chan', [(i, (i + by) % devices) for i in range(devic...  13.8 us
    ppermute x4, starting transfers between devices, onward(): return lax.ppermute(array, 'chan', pairs)  12.4 us
    ppermute x4, starting transfers between devices, shift(): lax.ppermute(array, 'chan', [(i, (i + by) % devices) for i in range(devic...  9.91 us
    pallas_call x1, Pallas kernels, shards(): pl.pallas_call(own_kernel, out_shape=[array(HELD, 2, dtype=jnp.float32)]...  7.35 us
    pallas_call x1, Pallas kernels, shards(): pl.pallas_call(diagonal_kernel, grid=(HELD, 2), out_shape=array(HELD, 2,...  7.13 us
    pallas_call x2, Pallas kernels, last(): pl.pallas_call(functools.partial(last_kernel, start, groups), out_shape=[...  5.53 us
    unnamed x16, local copies, waits for them, and re-layouts  5.07 us
  transfers between devices with their start and end apart: 9, of which 4 were waited for; matrix products, arithmetic and copies ran while one was open for 0% of the time, Pallas kernels for 31%

profile of v2, /device:TPU:7, one launch (start us, length us, event | category | flops | bytes accessed | tf_op | source)
XLA Modules:
  0.0 103.0 jit_solution(4708489943808600932)
XLA Ops:
  0.6 2.8 %head_kernel.1 = (bf16[4,2,2,128,384]{4,3,2,1,0:T(8,128)(2,1)}, bf16[4,2,2,128,384]{4,3,2,1,0:T(8,128)(2,1)}) custom-call(bf16[4,2,6,128,384]{4,3,2,1,0:T(8,128)(2,1)} %wave_ref.4), custom_call_target="tpu_custom_call" | custom-call | bytes 6000000 | tf_op jit(solution)/shard_map/head_kernel/pallas_call | solution.py:329
  3.4 1.4 %collective-permute-start.1 = (bf16[4,2,2,128,384]{4,3,2,1,0:T(8,128)(2,1)}, bf16[4,2,2,128,384]{4,3,2,1,0:T(8,128)(2,1)S(1)}, u32[]{:S(2)}, u32[]{:S(2)}) collective-permute-start(bf16[4,2,2,128,384]{4,3,2,1,0:T(8,128)(2,1)} %get-tuple-element.40), channel_id=1, source_target_pairs={{0,2},{2,4},{4,6},{6,8},{8,10},{10,12},{12,14},{14,16},{16,18},{18... | collective-permute-start | bytes 4718600 | tf_op jit(solution)/shard_map/ppermute | solution.py:319
  4.8 7.1 %collective-permute-start.2 = (bf16[4,2,2,128,384]{4,3,2,1,0:T(8,128)(2,1)}, bf16[4,2,2,128,384]{4,3,2,1,0:T(8,128)(2,1)S(1)}, u32[]{:S(2)}, u32[]{:S(2)}) collective-permute-start(bf16[4,2,2,128,384]{4,3,2,1,0:T(8,128)(2,1)} %get-tuple-element.58), channel_id=1, source_target_pairs={{0,254},{2,0},{4,2},{6,4},{8,6},{10,8},{12,10},{14,12},{16,14},{18... | collective-permute-start | bytes 4718600 | tf_op jit(solution)/shard_map/ppermute | solution.py:319
  11.9 4.1 %select_kernel.1 = (bf16[2,2,2,128,384]{4,3,2,1,0:T(8,128)(2,1)}, bf16[2,2,2,128,384]{4,3,2,1,0:T(8,128)(2,1)}, bf16[4,2,4,16,384]{4,3,2,1,0:T(8,128)(2,1)}) custom-call(s32[1]{0:T(128)} %bitcast.me_ref, s32[1]{0:T(128)} %bitcast.2.core_ref, s32[8,512]{1,0:T(8,128)} %bitcast.4, s32[512]{0:T(512)} %slots.3, bf16[4,2,6,128,384]{4,3,2,1,0:T(8,128)(2,1)} %wave_ref.4), custom_call_target="tpu_custom_call" | custom-call | bytes 9000000 | tf_op jit(solution)/shard_map/select_kernel/pallas_call | solution.py:341
  16.0 1.5 %collective-permute-start.6 = (bf16[2,2,2,128,384]{4,3,2,1,0:T(8,128)(2,1)}, bf16[2,2,2,128,384]{4,3,2,1,0:T(8,128)(2,1)}, u32[]{:S(2)}, u32[]{:S(2)}) collective-permute-start(bf16[2,2,2,128,384]{4,3,2,1,0:T(8,128)(2,1)} %get-tuple-element.62), channel_id=1, source_target_pairs={{0,254},{2,0},{4,2},{6,4},{8,6},{10,8},{12,10},{14,12},{16,14},{18... | collective-permute-start | bytes 2359304 | tf_op jit(solution)/shard_map/ppermute | solution.py:319
  17.4 1.5 %collective-permute-start = (bf16[4,2,4,16,384]{4,3,2,1,0:T(8,128)(2,1)}, bf16[4,2,4,16,384]{4,3,2,1,0:T(8,128)(2,1)S(1)}, u32[]{:S(2)}, u32[]{:S(2)}) collective-permute-start(bf16[4,2,4,16,384]{4,3,2,1,0:T(8,128)(2,1)} %get-tuple-element.52), channel_id=1, source_target_pairs={{0,1},{1,0},{2,3},{3,2},{4,5},{5,4},{6,7},{7,6},{8,9},{9,8},{10,11... | collective-permute-start | bytes 1179656 | tf_op jit(solution)/shard_map/ppermute | solution.py:354
  18.9 0.0 collective-permute-start.5
  18.9 0.7 copy-done.4
  19.6 0.7 copy-done.6
  20.3 0.7 copy-done.7
  21.0 4.5 %item_kernel.1 = (s32[5]{0:T(128)S(1)}, s32[5,32]{1,0:T(8,128)S(1)}, s32[8]{0:T(128)S(1)}) custom-call(s32[1]{0:T(128)} %bitcast.me_ref, s32[8,512]{1,0:T(8,128)S(1)} %bitcast.5, s32[512]{0:T(512)S(1)} %copy-done.4, s32[4,8]{1,0:T(4,128)S(1)} %copy-done.6, s32[4,8]{1,0:T(4,128)S(1)} %copy-done.7), custom_call_target="tpu_custom_call" | custom-call | bytes 18000000 | tf_op jit(solution)/shard_map/item_kernel/pallas_call | solution.py:356
  25.5 0.7 field_kernel.1
  26.3 0.0 collective-permute-done.edge_ref
  26.3 0.0 copy-start
  26.3 2.3 %copy-done = bf16[4,2,6,128,384]{4,3,2,1,0:T(8,128)(2,1)S(1)} copy-done((bf16[4,2,6,128,384]{4,3,2,1,0:T(8,128)(2,1)S(1)}, bf16[4,2,6,128,384]{4,3,2,1,0:T(8,128)(2,1)}, u32[]{:S(2)}) %copy-start) | copy-done | bytes 4718616
  28.6 0.7 copy-done.5
  29.3 7.1 %diagonal_kernel.1 = bf16[4,2,4,128,384]{4,3,2,1,0:T(8,128)(2,1)} custom-call(s32[1]{0:T(128)} %bitcast.1.row_ref, s32[4,3]{1,0:T(4,128)S(1)} %copy-done.5, bf16[4,2,6,128,384]{4,3,2,1,0:T(8,128)(2,1)S(1)} %copy-done, bf16[4,2,4,16,384]{4,3,2,1,0:T(8,128)(2,1)S(1)} %collective-permute-done.edge_ref), custom_call_target="tpu_custom_call" | custom-call | bytes 21000000 | tf_op jit(solution)/shard_map/diagonal_kernel/pallas_call | solution.py:381
  36.4 9.7 %collective-permute-done.1.all_ref.up_all = bf16[4,2,2,128,384]{4,3,2,1,0:T(8,128)(2,1)S(1)} collective-permute-done((bf16[4,2,2,128,384]{4,3,2,1,0:T(8,128)(2,1)}, bf16[4,2,2,128,384]{4,3,2,1,0:T(8,128)(2,1)S(1)}, u32[]{:S(2)}, u32[]{:S(2)}) %collective-permute-start.1) | collective-permute-done | bytes 1572896 | tf_op jit(solution)/shard_map/ppermute | solution.py:319
  46.1 0.7 pass_kernel.2
  46.8 0.7 pass_kernel.3
  47.5 6.7 %collective-permute-start.4 = (bf16[2,2,2,128,384]{4,3,2,1,0:T(8,128)(2,1)S(1)}, bf16[2,2,2,128,384]{4,3,2,1,0:T(8,128)(2,1)S(1)}, u32[]{:S(2)}, u32[]{:S(2)}) collective-permute-start(bf16[2,2,2,128,384]{4,3,2,1,0:T(8,128)(2,1)S(1)} %get-tuple-element.61), channel_id=1, source_target_pairs={{2,0},{4,2},{6,4},{8,6},{10,8},{12,10},{14,12},{16,14},{18,16},{20... | collective-permute-start | bytes 2359304 | tf_op jit(solution)/shard_map/ppermute | solution.py:327
  54.2 1.9 %collective-permute-start.8 = (bf16[2,2,2,128,384]{4,3,2,1,0:T(8,128)(2,1)S(1)}, bf16[2,2,2,128,384]{4,3,2,1,0:T(8,128)(2,1)S(1)}, u32[]{:S(2)}, u32[]{:S(2)}) collective-permute-start(bf16[2,2,2,128,384]{4,3,2,1,0:T(8,128)(2,1)S(1)} %get-tuple-element.71), channel_id=1, source_target_pairs={{0,250},{6,0},{8,2},{10,4},{12,6},{14,8},{16,10},{18,12},{20,14},{... | collective-permute-start | bytes 2359304 | tf_op jit(solution)/shard_map/ppermute | solution.py:327
  56.1 1.9 %collective-permute-start.7 = (bf16[2,2,2,128,384]{4,3,2,1,0:T(8,128)(2,1)S(1)}, bf16[2,2,2,128,384]{4,3,2,1,0:T(8,128)(2,1)S(1)}, u32[]{:S(2)}, u32[]{:S(2)}) collective-permute-start(bf16[2,2,2,128,384]{4,3,2,1,0:T(8,128)(2,1)S(1)} %get-tuple-element.56), channel_id=1, source_target_pairs={{2,4},{4,6},{6,8},{8,10},{10,12},{12,14},{14,16},{16,18},{18,20},{... | collective-permute-start | bytes 2359304 | tf_op jit(solution)/shard_map/ppermute | solution.py:327
  58.0 4.1 %collective-permute-done.6.down_two = bf16[2,2,2,128,384]{4,3,2,1,0:T(8,128)(2,1)} collective-permute-done((bf16[2,2,2,128,384]{4,3,2,1,0:T(8,128)(2,1)}, bf16[2,2,2,128,384]{4,3,2,1,0:T(8,128)(2,1)}, u32[]{:S(2)}, u32[]{:S(2)}) %collective-permute-start.6) | collective-permute-done | bytes 786464 | tf_op jit(solution)/shard_map/ppermute | solution.py:319
  62.1 1.9 %collective-permute-start.3 = (bf16[2,2,2,128,384]{4,3,2,1,0:T(8,128)(2,1)S(1)}, bf16[2,2,2,128,384]{4,3,2,1,0:T(8,128)(2,1)S(1)}, u32[]{:S(2)}, u32[]{:S(2)}) collective-permute-start(bf16[2,2,2,128,384]{4,3,2,1,0:T(8,128)(2,1)S(1)} %get-tuple-element.59), channel_id=1, source_target_pairs={{0,6},{2,8},{4,10},{6,12},{8,14},{10,16},{12,18},{14,20},{16,22},{... | collective-permute-start | bytes 2359304 | tf_op jit(solution)/shard_map/ppermute | solution.py:327
  64.1 7.3 %own_kernel.1 = (f32[4,2,128,384]{3,2,1,0:T(8,128)S(1)}, f32[4,2,128,384]{3,2,1,0:T(8,128)S(1)}, f32[4,2,128,384]{3,2,1,0:T(8,128)S(1)}, f32[4,2,128,384]{3,2,1,0:T(8,128)S(1)}) custom-call(s32[5]{0:T(128)S(1)} %get-tuple-element.45.count_ref, s32[5,32]{1,0:T(8,128)S(1)} %get-tuple-element.53.item_ref, f32[4,8]{1,0:T(4,128)S(1)} %copy-done.3, ...), custom_call_target="tpu_custom_call" | custom-call | bytes 27000000 | tf_op jit(solution)/shard_map/own_kernel/pallas_call | solution.py:416
  71.4 2.5 %near_kernel.1 = (f32[4,2,128,384]{3,2,1,0:T(8,128)S(1)}, f32[4,2,128,384]{3,2,1,0:T(8,128)S(1)}, f32[4,2,128,384]{3,2,1,0:T(8,128)S(1)}, f32[4,2,128,384]{3,2,1,0:T(8,128)S(1)}) custom-call(s32[5]{0:T(128)S(1)} %get-tuple-element.45.count_ref, ...), custom_call_target="tpu_custom_call", output_to_operand_aliasing={{0}: (9, {}), {1}: (10, {}), {2}: (11, {}), {3}: (12, {})} | custom-call | bytes 12000000 | tf_op jit(solution)/shard_map/near_kernel/pallas_call | solution.py:426
  73.9 16.6 %collective-permute-done.4.down_one = bf16[2,2,2,128,384]{4,3,2,1,0:T(8,128)(2,1)S(1)} collective-permute-done((bf16[2,2,2,128,384]{4,3,2,1,0:T(8,128)(2,1)S(1)}, bf16[2,2,2,128,384]{4,3,2,1,0:T(8,128)(2,1)S(1)}, u32[]{:S(2)}, u32[]{:S(2)}) %collective-permute-start.4) | collective-permute-done | bytes 786464 | tf_op jit(solution)/shard_map/ppermute | solution.py:327
  90.5 0.9 far_kernel.1
  91.5 6.0 %collective-permute-done.8.refs_1_ = bf16[2,2,2,128,384]{4,3,2,1,0:T(8,128)(2,1)S(1)} collective-permute-done((bf16[2,2,2,128,384]{4,3,2,1,0:T(8,128)(2,1)S(1)}, bf16[2,2,2,128,384]{4,3,2,1,0:T(8,128)(2,1)S(1)}, u32[]{:S(2)}, u32[]{:S(2)}) %collective-permute-start.8) | collective-permute-done | bytes 786464 | tf_op jit(solution)/shard_map/ppermute | solution.py:327
  97.4 2.9 %last_kernel.2 = (bf16[4,2,4,128,384]{4,3,2,1,0:T(8,128)(2,1)}, f32[4,2,128,384]{3,2,1,0:T(8,128)S(1)}, f32[4,2,128,384]{3,2,1,0:T(8,128)S(1)}) custom-call(s32[5]{0:T(128)S(1)} %get-tuple-element.45.count_ref, s32[5,32]{1,0:T(8,128)S(1)} %get-tuple-element.53.item_ref, f32[4,8]{1,0:T(4,128)S(1)} %copy-done.3, ...), custom_call_target="tpu_custom_call", output_to_operand_aliasing={{1}: (7, {}), {2}: (8, {})} | custom-call | bytes 6000000 | tf_op jit(solution)/shard_map/last_kernel/pallas_call | solution.py:454
  100.4 2.6 %last_kernel.3 = (bf16[4,2,4,128,384]{4,3,2,1,0:T(8,128)(2,1)}, f32[4,2,128,384]{3,2,1,0:T(8,128)S(1)}, f32[4,2,128,384]{3,2,1,0:T(8,128)S(1)}) custom-call(s32[5]{0:T(128)S(1)} %get-tuple-element.45.count_ref, s32[5,32]{1,0:T(8,128)S(1)} %get-tuple-element.53.item_ref, ...), custom_call_target="tpu_custom_call", output_to_operand_aliasing={{1}: (6, {}), {2}: (7, {}), {0}: (8, {})} | custom-call | bytes 6000000 | tf_op jit(solution)/shard_map/last_kernel/pallas_call | solution.py:454
  (14 shorter events, 0.0 us)
Async XLA Ops:
  3.4 42.7 %collective-permute-start.1 = (bf16[4,2,2,128,384]{4,3,2,1,0:T(8,128)(2,1)}, bf16[4,2,2,128,384]{4,3,2,1,0:T(8,128)(2,1)S(1)}, u32[]{:S(2)}, u32[]{:S(2)}) collective-permute-start(bf16[4,2,2,128,384]{4,3,2,1,0:T(8,128)(2,1)} %get-tuple-element.40), channel_id=1, source_target_pairs={{0,2},{2,4},{4,6},{6,8},{8,10},{10,12},{12,14},{14,16},{16,18},{18... | collective-permute-start | bytes 4718600 | tf_op jit(solution)/shard_map/ppermute | solution.py:319
  4.8 42.0 %collective-permute-start.2 = (bf16[4,2,2,128,384]{4,3,2,1,0:T(8,128)(2,1)}, bf16[4,2,2,128,384]{4,3,2,1,0:T(8,128)(2,1)S(1)}, u32[]{:S(2)}, u32[]{:S(2)}) collective-permute-start(bf16[4,2,2,128,384]{4,3,2,1,0:T(8,128)(2,1)} %get-tuple-element.58), channel_id=1, source_target_pairs={{0,254},{2,0},{4,2},{6,4},{8,6},{10,8},{12,10},{14,12},{16,14},{18... | collective-permute-start | bytes 4718600 | tf_op jit(solution)/shard_map/ppermute | solution.py:319
  11.9 7.1 %copy-start.2 = (s32[512,8]{0,1:T(8,128)S(1)}, s32[512,8]{0,1:T(8,128)}, u32[]{:S(2)}) copy-start(s32[512,8]{0,1:T(8,128)} %param.9) | copy-start | bytes 49156
  16.0 46.1 %collective-permute-start.6 = (bf16[2,2,2,128,384]{4,3,2,1,0:T(8,128)(2,1)}, bf16[2,2,2,128,384]{4,3,2,1,0:T(8,128)(2,1)}, u32[]{:S(2)}, u32[]{:S(2)}) collective-permute-start(bf16[2,2,2,128,384]{4,3,2,1,0:T(8,128)(2,1)} %get-tuple-element.62), channel_id=1, source_target_pairs={{0,254},{2,0},{4,2},{6,4},{8,6},{10,8},{12,10},{14,12},{16,14},{18... | collective-permute-start | bytes 2359304 | tf_op jit(solution)/shard_map/ppermute | solution.py:319
  17.4 8.8 %collective-permute-start = (bf16[4,2,4,16,384]{4,3,2,1,0:T(8,128)(2,1)}, bf16[4,2,4,16,384]{4,3,2,1,0:T(8,128)(2,1)S(1)}, u32[]{:S(2)}, u32[]{:S(2)}) collective-permute-start(bf16[4,2,4,16,384]{4,3,2,1,0:T(8,128)(2,1)} %get-tuple-element.52), channel_id=1, source_target_pairs={{0,1},{1,0},{2,3},{3,2},{4,5},{5,4},{6,7},{7,6},{8,9},{9,8},{10,11... | collective-permute-start | bytes 1179656 | tf_op jit(solution)/shard_map/ppermute | solution.py:354
  18.9 52.5 %collective-permute-start.5 = (bf16[2,2,2,128,384]{4,3,2,1,0:T(8,128)(2,1)}, bf16[2,2,2,128,384]{4,3,2,1,0:T(8,128)(2,1)}, u32[]{:S(2)}, u32[]{:S(2)}) collective-permute-start(bf16[2,2,2,128,384]{4,3,2,1,0:T(8,128)(2,1)} %get-tuple-element.42), channel_id=1, source_target_pairs={{0,2},{2,4},{4,6},{6,8},{8,10},{10,12},{12,14},{14,16},{16,18},{18... | collective-permute-start | bytes 2359304 | tf_op jit(solution)/shard_map/ppermute | solution.py:319
  18.9 0.7 copy-start.4
  19.6 0.7 copy-start.6
  20.3 0.7 copy-start.7
  26.3 2.3 %copy-start = (bf16[4,2,6,128,384]{4,3,2,1,0:T(8,128)(2,1)S(1)}, bf16[4,2,6,128,384]{4,3,2,1,0:T(8,128)(2,1)}, u32[]{:S(2)}) copy-start(bf16[4,2,6,128,384]{4,3,2,1,0:T(8,128)(2,1)} %wave_ref.4) | copy-start | bytes 14155780
  28.6 0.7 copy-start.5
  29.3 34.7 %copy-start.1 = (bf16[4,2,6,128,384]{4,3,2,1,0:T(8,128)(2,1)S(1)}, bf16[4,2,6,128,384]{4,3,2,1,0:T(8,128)(2,1)}, u32[]{:S(2)}) copy-start(bf16[4,2,6,128,384]{4,3,2,1,0:T(8,128)(2,1)} %wave_ref.4) | copy-start | bytes 14155780
  36.4 27.6 %copy-start.3 = (f32[4,8]{1,0:T(4,128)S(1)}, f32[4,8]{1,0:T(4,128)}, u32[]{:S(2)}) copy-start(f32[4,8]{1,0:T(4,128)} %weight_ref.4) | copy-start | bytes 388
  47.5 43.0 %collective-permute-start.4 = (bf16[2,2,2,128,384]{4,3,2,1,0:T(8,128)(2,1)S(1)}, bf16[2,2,2,128,384]{4,3,2,1,0:T(8,128)(2,1)S(1)}, u32[]{:S(2)}, u32[]{:S(2)}) collective-permute-start(bf16[2,2,2,128,384]{4,3,2,1,0:T(8,128)(2,1)S(1)} %get-tuple-element.61), channel_id=1, source_target_pairs={{2,0},{4,2},{6,4},{8,6},{10,8},{12,10},{14,12},{16,14},{18,16},{20... | collective-permute-start | bytes 2359304 | tf_op jit(solution)/shard_map/ppermute | solution.py:327
  54.2 43.2 %collective-permute-start.8 = (bf16[2,2,2,128,384]{4,3,2,1,0:T(8,128)(2,1)S(1)}, bf16[2,2,2,128,384]{4,3,2,1,0:T(8,128)(2,1)S(1)}, u32[]{:S(2)}, u32[]{:S(2)}) collective-permute-start(bf16[2,2,2,128,384]{4,3,2,1,0:T(8,128)(2,1)S(1)} %get-tuple-element.71), channel_id=1, source_target_pairs={{0,250},{6,0},{8,2},{10,4},{12,6},{14,8},{16,10},{18,12},{20,14},{... | collective-permute-start | bytes 2359304 | tf_op jit(solution)/shard_map/ppermute | solution.py:327
  56.1 41.3 %collective-permute-start.7 = (bf16[2,2,2,128,384]{4,3,2,1,0:T(8,128)(2,1)S(1)}, bf16[2,2,2,128,384]{4,3,2,1,0:T(8,128)(2,1)S(1)}, u32[]{:S(2)}, u32[]{:S(2)}) collective-permute-start(bf16[2,2,2,128,384]{4,3,2,1,0:T(8,128)(2,1)S(1)} %get-tuple-element.56), channel_id=1, source_target_pairs={{2,4},{4,6},{6,8},{8,10},{10,12},{12,14},{14,16},{16,18},{18,20},{... | collective-permute-start | bytes 2359304 | tf_op jit(solution)/shard_map/ppermute | solution.py:327
  62.1 38.2 %collective-permute-start.3 = (bf16[2,2,2,128,384]{4,3,2,1,0:T(8,128)(2,1)S(1)}, bf16[2,2,2,128,384]{4,3,2,1,0:T(8,128)(2,1)S(1)}, u32[]{:S(2)}, u32[]{:S(2)}) collective-permute-start(bf16[2,2,2,128,384]{4,3,2,1,0:T(8,128)(2,1)S(1)} %get-tuple-element.59), channel_id=1, source_target_pairs={{0,6},{2,8},{4,10},{6,12},{8,14},{10,16},{12,18},{14,20},{16,22},{... | collective-permute-start | bytes 2359304 | tf_op jit(solution)/shard_map/ppermute | solution.py:327

commit v3 on v2

--- a/solution.py
+++ b/solution.py
@@ -256,10 +256,11 @@
         add_items(group, True, p % HALF, count_ref, item_ref, weight_ref, fields[p], ref, totals[p])
 
 
-def far_kernel(count_ref, item_ref, weight_ref, down_one, *refs):
-    fields, totals = refs[:HALF], refs[-HALF:]
-    for p in range(HALF):
-        add_items(4, True, p, count_ref, item_ref, weight_ref, fields[p], down_one, totals[p])
+def far_kernel(count_ref, item_ref, weight_ref, up_one, down_one, *refs):
+    fields, totals = refs[:PLANES], refs[-PLANES:]
+    for p in range(PLANES):
+        group, ref = (3, up_one) if p < HALF else (4, down_one)
+        add_items(group, True, p % HALF, count_ref, item_ref, weight_ref, fields[p], ref, totals[p])
 
 
 def last_kernel(start, groups, count_ref, item_ref, weight_ref, *refs):
@@ -408,6 +409,7 @@
     up_one, down_three = passing(0, up_all, diag_step)
     down_one, up_three = passing(4, down_all, up_one)
     weights = behind(couple_weight, up_three)
+    down_three, up_three = behind(down_three, up_two), behind(up_three, down_two)
     moved = [
         onward(v, *where)
         for v, where in ((up_one, (-1, 1)), (down_three, (-1, -3)), (down_one, (1, -1)), (up_three, (1, 3)))
@@ -435,15 +437,15 @@
     )(*tables, up_two, down_two, *fields, *totals)
 
     up_one, down_three, down_one, up_three = moved
-    inputs = [*tables, down_one, *fields[HALF:], *totals[HALF:]]
-    late = pl.pallas_call(
+    inputs = [*tables, up_one, down_one, *fields, *totals]
+    totals = pl.pallas_call(
         far_kernel,
-        out_shape=[array(HELD, 2, dtype=jnp.float32)] * HALF,
+        out_shape=[array(HELD, 2, dtype=jnp.float32)] * PLANES,
         in_specs=[SMEM] * 3 + [VMEM] * (len(inputs) - 3),
-        out_specs=[VMEM] * HALF,
-        input_output_aliases={len(inputs) - HALF + p: p for p in range(HALF)},
+        out_specs=[VMEM] * PLANES,
+        input_output_aliases={len(inputs) - PLANES + p: p for p in range(PLANES)},
         compiler_params=params(8),
-        cost_estimate=cost(1),
+        cost_estimate=cost(2),
         name="far_kernel",
     )(*inputs)
 
@@ -463,9 +465,8 @@
             name="last_kernel",
         )(*inputs)[0]
 
-    soon = behind(totals[:HALF], late)
-    coupling = last(0, (3, 4), (up_one, down_three), soon)
-    coupling = last(HALF, (3,), (up_three,), late, coupling)
+    coupling = last(0, (4,), (down_three,), totals[:HALF])
+    coupling = last(HALF, (3,), (up_three,), totals[HALF:], coupling)
     return diag_step, coupling
 
 

time: 103 us -> 103 us (level)
  waiting for transfers between devices: 36.3 us -> 27.8 us
  starting transfers between devices: 23.8 us -> 31.7 us
    ppermute x4, waiting for transfers between devices: 22.5 us -> 16.4 us  [onward(): return lax.ppermute(array, 'chan', pairs)]
    ppermute x4, starting transfers between devices: 9.91 us -> 14.2 us  [shift(): lax.ppermute(array, 'chan', [(i, (i + by) % devices) for i in range(devic...]
    ppermute x4, starting transfers between devices: 12.4 us -> 16 us  [onward(): return lax.ppermute(array, 'chan', pairs)]
    ppermute x4, waiting for transfers between devices: 13.8 us -> 11.4 us  [shift(): lax.ppermute(array, 'chan', [(i, (i + by) % devices) for i in range(devic...]
    pallas_call x1, Pallas kernels: 0.95 us -> 2.21 us  [shards(): pl.pallas_call(far_kernel, out_shape=[array(HELD, 2, dtype=jnp.float32)]...]
  transfers between devices with their start and end apart: 9 -> 9, of which waited for: 4 -> 5; matrix products, arithmetic and copies ran while one was open for 0% -> 0% of each run, Pallas kernels for 31% -> 31%
where the time goes in v3:
time: 103 us; the launch traced here: 102 us
  Pallas kernels  37 us (36%)
  starting transfers between devices  31.7 us (31%)
  waiting for transfers between devices  27.8 us (27%)
  local copies, waits for them, and re-layouts  5.07 us (5%)
    ppermute x4, waiting for transfers between devices, onward(): return lax.ppermute(array, 'chan', pairs)  16.4 us
    ppermute x4, starting transfers between devices, onward(): return lax.ppermute(array, 'chan', pairs)  16 us
    ppermute x4, starting transfers between devices, shift(): lax.ppermute(array, 'chan', [(i, (i + by) % devices) for i in range(devic...  14.2 us
    ppermute x4, waiting for transfers between devices, shift(): lax.ppermute(array, 'chan', [(i, (i + by) % devices) for i in range(devic...  11.4 us
    pallas_call x1, Pallas kernels, shards(): pl.pallas_call(own_kernel, out_shape=[array(HELD, 2, dtype=jnp.float32)]...  7.47 us
    pallas_call x1, Pallas kernels, shards(): pl.pallas_call(diagonal_kernel, grid=(HELD, 2), out_shape=array(HELD, 2,...  7.13 us
    unnamed x16, local copies, waits for them, and re-layouts  5.07 us
    pallas_call x2, Pallas kernels, last(): pl.pallas_call(functools.partial(last_kernel, start, groups), out_shape=[...  4.92 us
  transfers between devices with their start and end apart: 9, of which 5 were waited for; matrix products, arithmetic and copies ran while one was open for 0% of the time, Pallas kernels for 31%

profile of v3, /device:TPU:7, one launch (start us, length us, event | category | flops | bytes accessed | tf_op | source)
XLA Modules:
  0.0 102.4 jit_solution(15073064756086720953)
XLA Ops:
  0.6 2.8 %head_kernel.1 = (bf16[4,2,2,128,384]{4,3,2,1,0:T(8,128)(2,1)}, bf16[4,2,2,128,384]{4,3,2,1,0:T(8,128)(2,1)}) custom-call(bf16[4,2,6,128,384]{4,3,2,1,0:T(8,128)(2,1)} %wave_ref.4), custom_call_target="tpu_custom_call" | custom-call | bytes 6000000 | tf_op jit(solution)/shard_map/head_kernel/pallas_call | solution.py:330
  3.4 1.4 %collective-permute-start.1 = (bf16[4,2,2,128,384]{4,3,2,1,0:T(8,128)(2,1)}, bf16[4,2,2,128,384]{4,3,2,1,0:T(8,128)(2,1)S(1)}, u32[]{:S(2)}, u32[]{:S(2)}) collective-permute-start(bf16[4,2,2,128,384]{4,3,2,1,0:T(8,128)(2,1)} %get-tuple-element.42), channel_id=1, source_target_pairs={{0,2},{2,4},{4,6},{6,8},{8,10},{10,12},{12,14},{14,16},{16,18},{18... | collective-permute-start | bytes 4718600 | tf_op jit(solution)/shard_map/ppermute | solution.py:320
  4.8 7.1 %collective-permute-start.2 = (bf16[4,2,2,128,384]{4,3,2,1,0:T(8,128)(2,1)}, bf16[4,2,2,128,384]{4,3,2,1,0:T(8,128)(2,1)S(1)}, u32[]{:S(2)}, u32[]{:S(2)}) collective-permute-start(bf16[4,2,2,128,384]{4,3,2,1,0:T(8,128)(2,1)} %get-tuple-element.60), channel_id=1, source_target_pairs={{0,254},{2,0},{4,2},{6,4},{8,6},{10,8},{12,10},{14,12},{16,14},{18... | collective-permute-start | bytes 4718600 | tf_op jit(solution)/shard_map/ppermute | solution.py:320
  11.9 4.1 %select_kernel.1 = (bf16[2,2,2,128,384]{4,3,2,1,0:T(8,128)(2,1)}, bf16[2,2,2,128,384]{4,3,2,1,0:T(8,128)(2,1)}, bf16[4,2,4,16,384]{4,3,2,1,0:T(8,128)(2,1)}) custom-call(s32[1]{0:T(128)} %bitcast.me_ref, s32[1]{0:T(128)} %bitcast.2.core_ref, s32[8,512]{1,0:T(8,128)} %bitcast.4, s32[512]{0:T(512)} %slots.3, bf16[4,2,6,128,384]{4,3,2,1,0:T(8,128)(2,1)} %wave_ref.4), custom_call_target="tpu_custom_call" | custom-call | bytes 9000000 | tf_op jit(solution)/shard_map/select_kernel/pallas_call | solution.py:342
  16.0 0.1 collective-permute-start.7
  16.1 5.7 %collective-permute-start.3 = (bf16[2,2,2,128,384]{4,3,2,1,0:T(8,128)(2,1)}, bf16[2,2,2,128,384]{4,3,2,1,0:T(8,128)(2,1)}, u32[]{:S(2)}, u32[]{:S(2)}) collective-permute-start(bf16[2,2,2,128,384]{4,3,2,1,0:T(8,128)(2,1)} %get-tuple-element.63), channel_id=1, source_target_pairs={{0,254},{2,0},{4,2},{6,4},{8,6},{10,8},{12,10},{14,12},{16,14},{18... | collective-permute-start | bytes 2359304 | tf_op jit(solution)/shard_map/ppermute | solution.py:320
  21.7 1.5 %collective-permute-start = (bf16[4,2,4,16,384]{4,3,2,1,0:T(8,128)(2,1)}, bf16[4,2,4,16,384]{4,3,2,1,0:T(8,128)(2,1)S(1)}, u32[]{:S(2)}, u32[]{:S(2)}) collective-permute-start(bf16[4,2,4,16,384]{4,3,2,1,0:T(8,128)(2,1)} %get-tuple-element.54), channel_id=1, source_target_pairs={{0,1},{1,0},{2,3},{3,2},{4,5},{5,4},{6,7},{7,6},{8,9},{9,8},{10,11... | collective-permute-start | bytes 1179656 | tf_op jit(solution)/shard_map/ppermute | solution.py:355
  23.3 0.7 copy-done.4
  23.9 0.7 copy-done.6
  24.6 0.7 copy-done.7
  25.3 4.5 %item_kernel.1 = (s32[5]{0:T(128)S(1)}, s32[5,32]{1,0:T(8,128)S(1)}, s32[8]{0:T(128)S(1)}) custom-call(s32[1]{0:T(128)} %bitcast.me_ref, s32[8,512]{1,0:T(8,128)S(1)} %bitcast.5, s32[512]{0:T(512)S(1)} %copy-done.4, s32[4,8]{1,0:T(4,128)S(1)} %copy-done.6, s32[4,8]{1,0:T(4,128)S(1)} %copy-done.7), custom_call_target="tpu_custom_call" | custom-call | bytes 18000000 | tf_op jit(solution)/shard_map/item_kernel/pallas_call | solution.py:357
  29.8 0.7 field_kernel.1
  30.6 0.0 copy-start
  30.6 2.3 %copy-done = bf16[4,2,6,128,384]{4,3,2,1,0:T(8,128)(2,1)S(1)} copy-done((bf16[4,2,6,128,384]{4,3,2,1,0:T(8,128)(2,1)S(1)}, bf16[4,2,6,128,384]{4,3,2,1,0:T(8,128)(2,1)}, u32[]{:S(2)}) %copy-start) | copy-done | bytes 4718616
  32.9 0.7 copy-done.5
  33.6 7.1 %diagonal_kernel.1 = bf16[4,2,4,128,384]{4,3,2,1,0:T(8,128)(2,1)} custom-call(s32[1]{0:T(128)} %bitcast.1.row_ref, s32[4,3]{1,0:T(4,128)S(1)} %copy-done.5, bf16[4,2,6,128,384]{4,3,2,1,0:T(8,128)(2,1)S(1)} %copy-done, bf16[4,2,4,16,384]{4,3,2,1,0:T(8,128)(2,1)S(1)} %collective-permute-done.edge_ref), custom_call_target="tpu_custom_call" | custom-call | bytes 21000000 | tf_op jit(solution)/shard_map/diagonal_kernel/pallas_call | solution.py:382
  40.7 5.4 %collective-permute-done.1.all_ref.up_all = bf16[4,2,2,128,384]{4,3,2,1,0:T(8,128)(2,1)S(1)} collective-permute-done((bf16[4,2,2,128,384]{4,3,2,1,0:T(8,128)(2,1)}, bf16[4,2,2,128,384]{4,3,2,1,0:T(8,128)(2,1)S(1)}, u32[]{:S(2)}, u32[]{:S(2)}) %collective-permute-start.1) | collective-permute-done | bytes 1572896 | tf_op jit(solution)/shard_map/ppermute | solution.py:320
  46.1 0.7 pass_kernel.2
  46.8 1.9 %collective-permute-start.5 = (bf16[2,2,2,128,384]{4,3,2,1,0:T(8,128)(2,1)S(1)}, bf16[2,2,2,128,384]{4,3,2,1,0:T(8,128)(2,1)S(1)}, u32[]{:S(2)}, u32[]{:S(2)}) collective-permute-start(bf16[2,2,2,128,384]{4,3,2,1,0:T(8,128)(2,1)S(1)} %get-tuple-element.58), channel_id=1, source_target_pairs={{2,4},{4,6},{6,8},{8,10},{10,12},{12,14},{14,16},{16,18},{18,20},{... | collective-permute-start | bytes 2359304 | tf_op jit(solution)/shard_map/ppermute | solution.py:328
  48.8 0.7 pass_kernel.3
  49.4 7.6 %collective-permute-start.6 = (bf16[2,2,2,128,384]{4,3,2,1,0:T(8,128)(2,1)S(1)}, bf16[2,2,2,128,384]{4,3,2,1,0:T(8,128)(2,1)S(1)}, u32[]{:S(2)}, u32[]{:S(2)}) collective-permute-start(bf16[2,2,2,128,384]{4,3,2,1,0:T(8,128)(2,1)S(1)} %get-tuple-element.65), channel_id=1, source_target_pairs={{2,0},{4,2},{6,4},{8,6},{10,8},{12,10},{14,12},{16,14},{18,16},{20... | collective-permute-start | bytes 2359304 | tf_op jit(solution)/shard_map/ppermute | solution.py:328
  57.0 6.1 %collective-permute-done.7.up_two = bf16[2,2,2,128,384]{4,3,2,1,0:T(8,128)(2,1)} collective-permute-done((bf16[2,2,2,128,384]{4,3,2,1,0:T(8,128)(2,1)}, bf16[2,2,2,128,384]{4,3,2,1,0:T(8,128)(2,1)}, u32[]{:S(2)}, u32[]{:S(2)}) %collective-permute-start.7) | collective-permute-done | bytes 786464 | tf_op jit(solution)/shard_map/ppermute | solution.py:320
  63.1 1.9 %collective-permute-start.8 = (bf16[2,2,2,128,384]{4,3,2,1,0:T(8,128)(2,1)S(1)}, bf16[2,2,2,128,384]{4,3,2,1,0:T(8,128)(2,1)S(1)}, u32[]{:S(2)}, u32[]{:S(2)}) collective-permute-start(bf16[2,2,2,128,384]{4,3,2,1,0:T(8,128)(2,1)S(1)} %get-tuple-element.77), channel_id=1, source_target_pairs={{0,250},{6,0},{8,2},{10,4},{12,6},{14,8},{16,10},{18,12},{20,14},{... | collective-permute-start | bytes 2359304 | tf_op jit(solution)/shard_map/ppermute | solution.py:328
  65.0 4.6 %collective-permute-start.4 = (bf16[2,2,2,128,384]{4,3,2,1,0:T(8,128)(2,1)S(1)}, bf16[2,2,2,128,384]{4,3,2,1,0:T(8,128)(2,1)S(1)}, u32[]{:S(2)}, u32[]{:S(2)}) collective-permute-start(bf16[2,2,2,128,384]{4,3,2,1,0:T(8,128)(2,1)S(1)} %get-tuple-element.64), channel_id=1, source_target_pairs={{0,6},{2,8},{4,10},{6,12},{8,14},{10,16},{12,18},{14,20},{16,22},{... | collective-permute-start | bytes 2359304 | tf_op jit(solution)/shard_map/ppermute | solution.py:328
  69.6 7.5 %own_kernel.1 = (f32[4,2,128,384]{3,2,1,0:T(8,128)S(1)}, f32[4,2,128,384]{3,2,1,0:T(8,128)S(1)}, f32[4,2,128,384]{3,2,1,0:T(8,128)S(1)}, f32[4,2,128,384]{3,2,1,0:T(8,128)S(1)}) custom-call(s32[5]{0:T(128)S(1)} %get-tuple-element.47.count_ref, s32[5,32]{1,0:T(8,128)S(1)} %get-tuple-element.55.item_ref, f32[4,8]{1,0:T(4,128)S(1)} %copy-done.3, ...), custom_call_target="tpu_custom_call" | custom-call | bytes 27000000 | tf_op jit(solution)/shard_map/own_kernel/pallas_call | solution.py:418
  77.1 1.7 %near_kernel.1 = (f32[4,2,128,384]{3,2,1,0:T(8,128)S(1)}, f32[4,2,128,384]{3,2,1,0:T(8,128)S(1)}, f32[4,2,128,384]{3,2,1,0:T(8,128)S(1)}, f32[4,2,128,384]{3,2,1,0:T(8,128)S(1)}) custom-call(s32[5]{0:T(128)S(1)} %get-tuple-element.47.count_ref, ...), custom_call_target="tpu_custom_call", output_to_operand_aliasing={{0}: (9, {}), {1}: (10, {}), {2}: (11, {}), {3}: (12, {})} | custom-call | bytes 12000000 | tf_op jit(solution)/shard_map/near_kernel/pallas_call | solution.py:428
  78.8 1.0 collective-permute-done.5.up_one
  79.8 10.7 %collective-permute-done.6.down_one = bf16[2,2,2,128,384]{4,3,2,1,0:T(8,128)(2,1)S(1)} collective-permute-done((bf16[2,2,2,128,384]{4,3,2,1,0:T(8,128)(2,1)S(1)}, bf16[2,2,2,128,384]{4,3,2,1,0:T(8,128)(2,1)S(1)}, u32[]{:S(2)}, u32[]{:S(2)}) %collective-permute-start.6) | collective-permute-done | bytes 786464 | tf_op jit(solution)/shard_map/ppermute | solution.py:328
  90.5 2.2 %far_kernel.1 = (f32[4,2,128,384]{3,2,1,0:T(8,128)S(1)}, f32[4,2,128,384]{3,2,1,0:T(8,128)S(1)}, f32[4,2,128,384]{3,2,1,0:T(8,128)S(1)}, f32[4,2,128,384]{3,2,1,0:T(8,128)S(1)}) custom-call(s32[5]{0:T(128)S(1)} %get-tuple-element.47.count_ref, ...), custom_call_target="tpu_custom_call", output_to_operand_aliasing={{0}: (9, {}), {1}: (10, {}), {2}: (11, {}), {3}: (12, {})} | custom-call | bytes 6000000 | tf_op jit(solution)/shard_map/far_kernel/pallas_call | solution.py:441
  92.7 4.7 %collective-permute-done.8.refs_0_ = bf16[2,2,2,128,384]{4,3,2,1,0:T(8,128)(2,1)S(1)} collective-permute-done((bf16[2,2,2,128,384]{4,3,2,1,0:T(8,128)(2,1)S(1)}, bf16[2,2,2,128,384]{4,3,2,1,0:T(8,128)(2,1)S(1)}, u32[]{:S(2)}, u32[]{:S(2)}) %collective-permute-start.8) | collective-permute-done | bytes 786464 | tf_op jit(solution)/shard_map/ppermute | solution.py:328
  97.4 2.5 %last_kernel.2 = (bf16[4,2,4,128,384]{4,3,2,1,0:T(8,128)(2,1)}, f32[4,2,128,384]{3,2,1,0:T(8,128)S(1)}, f32[4,2,128,384]{3,2,1,0:T(8,128)S(1)}) custom-call(s32[5]{0:T(128)S(1)} %get-tuple-element.47.count_ref, s32[5,32]{1,0:T(8,128)S(1)} %get-tuple-element.55.item_ref, f32[4,8]{1,0:T(4,128)S(1)} %copy-done.3, ...), custom_call_target="tpu_custom_call", output_to_operand_aliasing={{1}: (6, {}), {2}: (7, {})} | custom-call | bytes 6000000 | tf_op jit(solution)/shard_map/last_kernel/pallas_call | solution.py:456
  99.9 2.5 %last_kernel.3 = (bf16[4,2,4,128,384]{4,3,2,1,0:T(8,128)(2,1)}, f32[4,2,128,384]{3,2,1,0:T(8,128)S(1)}, f32[4,2,128,384]{3,2,1,0:T(8,128)S(1)}) custom-call(s32[5]{0:T(128)S(1)} %get-tuple-element.47.count_ref, s32[5,32]{1,0:T(8,128)S(1)} %get-tuple-element.55.item_ref, ...), custom_call_target="tpu_custom_call", output_to_operand_aliasing={{1}: (6, {}), {2}: (7, {}), {0}: (8, {})} | custom-call | bytes 6000000 | tf_op jit(solution)/shard_map/last_kernel/pallas_call | solution.py:456
  (14 shorter events, 0.0 us)
Async XLA Ops:
  3.4 42.7 %collective-permute-start.1 = (bf16[4,2,2,128,384]{4,3,2,1,0:T(8,128)(2,1)}, bf16[4,2,2,128,384]{4,3,2,1,0:T(8,128)(2,1)S(1)}, u32[]{:S(2)}, u32[]{:S(2)}) collective-permute-start(bf16[4,2,2,128,384]{4,3,2,1,0:T(8,128)(2,1)} %get-tuple-element.42), channel_id=1, source_target_pairs={{0,2},{2,4},{4,6},{6,8},{8,10},{10,12},{12,14},{14,16},{16,18},{18... | collective-permute-start | bytes 4718600 | tf_op jit(solution)/shard_map/ppermute | solution.py:320
  4.8 43.9 %collective-permute-start.2 = (bf16[4,2,2,128,384]{4,3,2,1,0:T(8,128)(2,1)}, bf16[4,2,2,128,384]{4,3,2,1,0:T(8,128)(2,1)S(1)}, u32[]{:S(2)}, u32[]{:S(2)}) collective-permute-start(bf16[4,2,2,128,384]{4,3,2,1,0:T(8,128)(2,1)} %get-tuple-element.60), channel_id=1, source_target_pairs={{0,254},{2,0},{4,2},{6,4},{8,6},{10,8},{12,10},{14,12},{16,14},{18... | collective-permute-start | bytes 4718600 | tf_op jit(solution)/shard_map/ppermute | solution.py:320
  11.9 11.4 %copy-start.2 = (s32[512,8]{0,1:T(8,128)S(1)}, s32[512,8]{0,1:T(8,128)}, u32[]{:S(2)}) copy-start(s32[512,8]{0,1:T(8,128)} %param.9) | copy-start | bytes 49156
  16.0 47.1 %collective-permute-start.7 = (bf16[2,2,2,128,384]{4,3,2,1,0:T(8,128)(2,1)}, bf16[2,2,2,128,384]{4,3,2,1,0:T(8,128)(2,1)}, u32[]{:S(2)}, u32[]{:S(2)}) collective-permute-start(bf16[2,2,2,128,384]{4,3,2,1,0:T(8,128)(2,1)} %get-tuple-element.44), channel_id=1, source_target_pairs={{0,2},{2,4},{4,6},{6,8},{8,10},{10,12},{12,14},{14,16},{16,18},{18... | collective-permute-start | bytes 2359304 | tf_op jit(solution)/shard_map/ppermute | solution.py:320
  16.1 48.9 %collective-permute-start.3 = (bf16[2,2,2,128,384]{4,3,2,1,0:T(8,128)(2,1)}, bf16[2,2,2,128,384]{4,3,2,1,0:T(8,128)(2,1)}, u32[]{:S(2)}, u32[]{:S(2)}) collective-permute-start(bf16[2,2,2,128,384]{4,3,2,1,0:T(8,128)(2,1)} %get-tuple-element.63), channel_id=1, source_target_pairs={{0,254},{2,0},{4,2},{6,4},{8,6},{10,8},{12,10},{14,12},{16,14},{18... | collective-permute-start | bytes 2359304 | tf_op jit(solution)/shard_map/ppermute | solution.py:320
  21.7 8.8 %collective-permute-start = (bf16[4,2,4,16,384]{4,3,2,1,0:T(8,128)(2,1)}, bf16[4,2,4,16,384]{4,3,2,1,0:T(8,128)(2,1)S(1)}, u32[]{:S(2)}, u32[]{:S(2)}) collective-permute-start(bf16[4,2,4,16,384]{4,3,2,1,0:T(8,128)(2,1)} %get-tuple-element.54), channel_id=1, source_target_pairs={{0,1},{1,0},{2,3},{3,2},{4,5},{5,4},{6,7},{7,6},{8,9},{9,8},{10,11... | collective-permute-start | bytes 1179656 | tf_op jit(solution)/shard_map/ppermute | solution.py:355
  23.3 0.7 copy-start.4
  23.9 0.7 copy-start.6
  24.6 0.7 copy-start.7
  30.6 2.3 %copy-start = (bf16[4,2,6,128,384]{4,3,2,1,0:T(8,128)(2,1)S(1)}, bf16[4,2,6,128,384]{4,3,2,1,0:T(8,128)(2,1)}, u32[]{:S(2)}) copy-start(bf16[4,2,6,128,384]{4,3,2,1,0:T(8,128)(2,1)} %wave_ref.4) | copy-start | bytes 14155780
  32.9 0.7 copy-start.5
  33.6 36.0 %copy-start.1 = (bf16[4,2,6,128,384]{4,3,2,1,0:T(8,128)(2,1)S(1)}, bf16[4,2,6,128,384]{4,3,2,1,0:T(8,128)(2,1)}, u32[]{:S(2)}) copy-start(bf16[4,2,6,128,384]{4,3,2,1,0:T(8,128)(2,1)} %wave_ref.4) | copy-start | bytes 14155780
  40.7 28.9 %copy-start.3 = (f32[4,8]{1,0:T(4,128)S(1)}, f32[4,8]{1,0:T(4,128)}, u32[]{:S(2)}) copy-start(f32[4,8]{1,0:T(4,128)} %weight_ref.4) | copy-start | bytes 388
  46.8 33.0 %collective-permute-start.5 = (bf16[2,2,2,128,384]{4,3,2,1,0:T(8,128)(2,1)S(1)}, bf16[2,2,2,128,384]{4,3,2,1,0:T(8,128)(2,1)S(1)}, u32[]{:S(2)}, u32[]{:S(2)}) collective-permute-start(bf16[2,2,2,128,384]{4,3,2,1,0:T(8,128)(2,1)S(1)} %get-tuple-element.58), channel_id=1, source_target_pairs={{2,4},{4,6},{6,8},{8,10},{10,12},{12,14},{14,16},{16,18},{18,20},{... | collective-permute-start | bytes 2359304 | tf_op jit(solution)/shard_map/ppermute | solution.py:328
  49.4 41.1 %collective-permute-start.6 = (bf16[2,2,2,128,384]{4,3,2,1,0:T(8,128)(2,1)S(1)}, bf16[2,2,2,128,384]{4,3,2,1,0:T(8,128)(2,1)S(1)}, u32[]{:S(2)}, u32[]{:S(2)}) collective-permute-start(bf16[2,2,2,128,384]{4,3,2,1,0:T(8,128)(2,1)S(1)} %get-tuple-element.65), channel_id=1, source_target_pairs={{2,0},{4,2},{6,4},{8,6},{10,8},{12,10},{14,12},{16,14},{18,16},{20... | collective-permute-start | bytes 2359304 | tf_op jit(solution)/shard_map/ppermute | solution.py:328
  63.1 34.3 %collective-permute-start.8 = (bf16[2,2,2,128,384]{4,3,2,1,0:T(8,128)(2,1)S(1)}, bf16[2,2,2,128,384]{4,3,2,1,0:T(8,128)(2,1)S(1)}, u32[]{:S(2)}, u32[]{:S(2)}) collective-permute-start(bf16[2,2,2,128,384]{4,3,2,1,0:T(8,128)(2,1)S(1)} %get-tuple-element.77), channel_id=1, source_target_pairs={{0,250},{6,0},{8,2},{10,4},{12,6},{14,8},{16,10},{18,12},{20,14},{... | collective-permute-start | bytes 2359304 | tf_op jit(solution)/shard_map/ppermute | solution.py:328
  65.0 34.9 %collective-permute-start.4 = (bf16[2,2,2,128,384]{4,3,2,1,0:T(8,128)(2,1)S(1)}, bf16[2,2,2,128,384]{4,3,2,1,0:T(8,128)(2,1)S(1)}, u32[]{:S(2)}, u32[]{:S(2)}) collective-permute-start(bf16[2,2,2,128,384]{4,3,2,1,0:T(8,128)(2,1)S(1)} %get-tuple-element.64), channel_id=1, source_target_pairs={{0,6},{2,8},{4,10},{6,12},{8,14},{10,16},{12,18},{14,20},{16,22},{... | collective-permute-start | bytes 2359304 | tf_op jit(solution)/shard_map/ppermute | solution.py:328

commit v4 on v3

--- a/solution.py
+++ b/solution.py
@@ -124,8 +124,10 @@
         pass_ref[2 * i + 1] = pair[1]
     firsts = [needed(source_ref, slot_ref, other(by), -by, devices)[0] for by in (-1, 1, -2, 2)]
     for g in range(GROUPS):
-        count_ref[g] = jnp.int32(0)
+        count_ref[g, HELD] = jnp.int32(0)
     for s in range(HELD):
+        for g in range(GROUPS):
+            count_ref[g, s] = count_ref[g, HELD]
         for e in range(PARTS):
             slot = slot_ref[source_ref[e, me * HELD + s]]
             local, offset = slot % HELD, slot // HELD - me
@@ -135,9 +137,9 @@
                 first = jnp.where(offset == by, firsts[g], first)
             place = jnp.where(local == first, 0, 1)
             field = pair_ref[s, e] * ORDERS + order_ref[s, e]
-            number = count_ref[group]
+            number = count_ref[group, HELD]
             item_ref[group, number] = (s * PARTS + e) + ENTRIES * (local + HELD * (place + 2 * field))
-            count_ref[group] = number + 1
+            count_ref[group, HELD] = number + 1
 
 
 def pass_kernel(first, pass_ref, all_ref, one_ref, three_ref):
@@ -213,7 +215,7 @@
         out_ref[0, 0, p] = (sign * energy).astype(out_ref.dtype)
 
 
-def add_items(group, selected, p, count_ref, item_ref, weight_ref, field_ref, source_ref, total):
+def add_items(group, selected, p, count_ref, item_ref, weight_ref, field_ref, source_ref, total, channel=None):
     rows = total.shape[2]
     step = 16
 
@@ -232,7 +234,9 @@
                 total[s, c, at] += factor * source_ref[place, c, p, at].astype(jnp.float32)
         return carry
 
-    lax.fori_loop(0, count_ref[group], one, 0)
+    begin = 0 if channel is None else count_ref[group, channel]
+    end = count_ref[group, HELD if channel is None else channel + 1]
+    lax.fori_loop(begin, end, one, 0)
 
 
 def own_kernel(count_ref, item_ref, weight_ref, wave_ref, up_all, down_all, *refs):
@@ -268,9 +272,9 @@
     totals, out_ref, (staged, sem) = refs[-2 - HALF : -2], refs[-3 - HALF], refs[-2:]
     copies = []
     for p, total in enumerate(totals):
-        for group, ref in zip(groups, fars):
-            add_items(group, True, p, count_ref, item_ref, weight_ref, fields[p], ref, total)
         for s in range(HELD):
+            for group, ref in zip(groups, fars):
+                add_items(group, True, p, count_ref, item_ref, weight_ref, fields[p], ref, total, s)
             staged[p, s, 0] = total[s, 1].astype(staged.dtype)
             staged[p, s, 1] = (-total[s, 0]).astype(staged.dtype)
             copies.append(
@@ -357,7 +361,7 @@
     count, item, passed = pl.pallas_call(
         functools.partial(item_kernel, devices),
         out_shape=(
-            jax.ShapeDtypeStruct((GROUPS,), jnp.int32),
+            jax.ShapeDtypeStruct((GROUPS, HELD + 1), jnp.int32),
             jax.ShapeDtypeStruct((GROUPS, ENTRIES), jnp.int32),
             jax.ShapeDtypeStruct((8,), jnp.int32),
         ),

time: 103 us -> 102 us (level)
    pallas_call x1, Pallas kernels: 1.73 us -> 2.82 us  [shards(): pl.pallas_call(near_kernel, out_shape=[array(HELD, 2, dtype=jnp.float32)]...]
  transfers between devices with their start and end apart: 9 -> 9, of which waited for: 5 -> 4; matrix products, arithmetic and copies ran while one was open for 0% -> 0% of each run, Pallas kernels for 31% -> 32%
where the time goes in v4:
time: 102 us
  Pallas kernels  37.1 us (36%)
  starting transfers between devices  31.7 us (31%)
  waiting for transfers between devices  27 us (26%)
  local copies, waits for them, and re-layouts  5.07 us (5%)
    ppermute x4, starting transfers between devices, onward(): return lax.ppermute(array, 'chan', pairs)  16 us
    ppermute x4, waiting for transfers between devices, onward(): return lax.ppermute(array, 'chan', pairs)  15.6 us
    ppermute x4, starting transfers between devices, shift(): lax.ppermute(array, 'chan', [(i, (i + by) % devices) for i in range(devic...  14.2 us
    ppermute x4, waiting for transfers between devices, shift(): lax.ppermute(array, 'chan', [(i, (i + by) % devices) for i in range(devic...  11.4 us
    pallas_call x1, Pallas kernels, shards(): pl.pallas_call(own_kernel, out_shape=[array(HELD, 2, dtype=jnp.float32)]...  7.71 us
    pallas_call x1, Pallas kernels, shards(): pl.pallas_call(diagonal_kernel, grid=(HELD, 2), out_shape=array(HELD, 2,...  7.13 us
    unnamed x16, local copies, waits for them, and re-layouts  5.07 us
    pallas_call x1, Pallas kernels, shards(): pl.pallas_call(functools.partial(item_kernel, devices), out_shape=(jax.Sh...  4.6 us
  transfers between devices with their start and end apart: 9, of which 4 were waited for; matrix products, arithmetic and copies ran while one was open for 0% of the time, Pallas kernels for 32%

profile of v4, /device:TPU:7, one launch (start us, length us, event | category | flops | bytes accessed | tf_op | source)
XLA Modules:
  0.0 101.7 jit_solution(13230282671591344938)
XLA Ops:
  0.6 2.8 %head_kernel.1 = (bf16[4,2,2,128,384]{4,3,2,1,0:T(8,128)(2,1)}, bf16[4,2,2,128,384]{4,3,2,1,0:T(8,128)(2,1)}) custom-call(bf16[4,2,6,128,384]{4,3,2,1,0:T(8,128)(2,1)} %wave_ref.4), custom_call_target="tpu_custom_call" | custom-call | bytes 6000000 | tf_op jit(solution)/shard_map/head_kernel/pallas_call | solution.py:334
  3.4 1.4 %collective-permute-start.1 = (bf16[4,2,2,128,384]{4,3,2,1,0:T(8,128)(2,1)}, bf16[4,2,2,128,384]{4,3,2,1,0:T(8,128)(2,1)S(1)}, u32[]{:S(2)}, u32[]{:S(2)}) collective-permute-start(bf16[4,2,2,128,384]{4,3,2,1,0:T(8,128)(2,1)} %get-tuple-element.42), channel_id=1, source_target_pairs={{0,2},{2,4},{4,6},{6,8},{8,10},{10,12},{12,14},{14,16},{16,18},{18... | collective-permute-start | bytes 4718600 | tf_op jit(solution)/shard_map/ppermute | solution.py:324
  4.8 7.1 %collective-permute-start.2 = (bf16[4,2,2,128,384]{4,3,2,1,0:T(8,128)(2,1)}, bf16[4,2,2,128,384]{4,3,2,1,0:T(8,128)(2,1)S(1)}, u32[]{:S(2)}, u32[]{:S(2)}) collective-permute-start(bf16[4,2,2,128,384]{4,3,2,1,0:T(8,128)(2,1)} %get-tuple-element.60), channel_id=1, source_target_pairs={{0,254},{2,0},{4,2},{6,4},{8,6},{10,8},{12,10},{14,12},{16,14},{18... | collective-permute-start | bytes 4718600 | tf_op jit(solution)/shard_map/ppermute | solution.py:324
  11.9 4.1 %select_kernel.1 = (bf16[2,2,2,128,384]{4,3,2,1,0:T(8,128)(2,1)}, bf16[2,2,2,128,384]{4,3,2,1,0:T(8,128)(2,1)}, bf16[4,2,4,16,384]{4,3,2,1,0:T(8,128)(2,1)}) custom-call(s32[1]{0:T(128)} %bitcast.me_ref, s32[1]{0:T(128)} %bitcast.2.core_ref, s32[8,512]{1,0:T(8,128)} %bitcast.4, s32[512]{0:T(512)} %slots.3, bf16[4,2,6,128,384]{4,3,2,1,0:T(8,128)(2,1)} %wave_ref.4), custom_call_target="tpu_custom_call" | custom-call | bytes 9000000 | tf_op jit(solution)/shard_map/select_kernel/pallas_call | solution.py:346
  16.0 0.1 collective-permute-start.7
  16.1 5.7 %collective-permute-start.3 = (bf16[2,2,2,128,384]{4,3,2,1,0:T(8,128)(2,1)}, bf16[2,2,2,128,384]{4,3,2,1,0:T(8,128)(2,1)}, u32[]{:S(2)}, u32[]{:S(2)}) collective-permute-start(bf16[2,2,2,128,384]{4,3,2,1,0:T(8,128)(2,1)} %get-tuple-element.63), channel_id=1, source_target_pairs={{0,254},{2,0},{4,2},{6,4},{8,6},{10,8},{12,10},{14,12},{16,14},{18... | collective-permute-start | bytes 2359304 | tf_op jit(solution)/shard_map/ppermute | solution.py:324
  21.7 1.5 %collective-permute-start = (bf16[4,2,4,16,384]{4,3,2,1,0:T(8,128)(2,1)}, bf16[4,2,4,16,384]{4,3,2,1,0:T(8,128)(2,1)S(1)}, u32[]{:S(2)}, u32[]{:S(2)}) collective-permute-start(bf16[4,2,4,16,384]{4,3,2,1,0:T(8,128)(2,1)} %get-tuple-element.54), channel_id=1, source_target_pairs={{0,1},{1,0},{2,3},{3,2},{4,5},{5,4},{6,7},{7,6},{8,9},{9,8},{10,11... | collective-permute-start | bytes 1179656 | tf_op jit(solution)/shard_map/ppermute | solution.py:359
  23.3 0.7 copy-done.4
  23.9 0.7 copy-done.6
  24.6 0.7 copy-done.7
  25.3 4.6 %item_kernel.1 = (s32[5,5]{1,0:T(8,128)S(1)}, s32[5,32]{1,0:T(8,128)S(1)}, s32[8]{0:T(128)S(1)}) custom-call(s32[1]{0:T(128)} %bitcast.me_ref, s32[8,512]{1,0:T(8,128)S(1)} %bitcast.5, s32[512]{0:T(512)S(1)} %copy-done.4, s32[4,8]{1,0:T(4,128)S(1)} %copy-done.6, s32[4,8]{1,0:T(4,128)S(1)} %copy-done.7), custom_call_target="tpu_custom_call" | custom-call | bytes 18000000 | tf_op jit(solution)/shard_map/item_kernel/pallas_call | solution.py:361
  29.9 0.7 field_kernel.1
  30.7 0.0 copy-start
  30.7 2.3 %copy-done = bf16[4,2,6,128,384]{4,3,2,1,0:T(8,128)(2,1)S(1)} copy-done((bf16[4,2,6,128,384]{4,3,2,1,0:T(8,128)(2,1)S(1)}, bf16[4,2,6,128,384]{4,3,2,1,0:T(8,128)(2,1)}, u32[]{:S(2)}) %copy-start) | copy-done | bytes 4718616
  33.0 0.7 copy-done.5
  33.7 7.1 %diagonal_kernel.1 = bf16[4,2,4,128,384]{4,3,2,1,0:T(8,128)(2,1)} custom-call(s32[1]{0:T(128)} %bitcast.1.row_ref, s32[4,3]{1,0:T(4,128)S(1)} %copy-done.5, bf16[4,2,6,128,384]{4,3,2,1,0:T(8,128)(2,1)S(1)} %copy-done, bf16[4,2,4,16,384]{4,3,2,1,0:T(8,128)(2,1)S(1)} %collective-permute-done.edge_ref), custom_call_target="tpu_custom_call" | custom-call | bytes 21000000 | tf_op jit(solution)/shard_map/diagonal_kernel/pallas_call | solution.py:386
  40.8 5.3 %collective-permute-done.1.all_ref.up_all = bf16[4,2,2,128,384]{4,3,2,1,0:T(8,128)(2,1)S(1)} collective-permute-done((bf16[4,2,2,128,384]{4,3,2,1,0:T(8,128)(2,1)}, bf16[4,2,2,128,384]{4,3,2,1,0:T(8,128)(2,1)S(1)}, u32[]{:S(2)}, u32[]{:S(2)}) %collective-permute-start.1) | collective-permute-done | bytes 1572896 | tf_op jit(solution)/shard_map/ppermute | solution.py:324
  46.1 0.7 pass_kernel.2
  46.8 1.9 %collective-permute-start.5 = (bf16[2,2,2,128,384]{4,3,2,1,0:T(8,128)(2,1)S(1)}, bf16[2,2,2,128,384]{4,3,2,1,0:T(8,128)(2,1)S(1)}, u32[]{:S(2)}, u32[]{:S(2)}) collective-permute-start(bf16[2,2,2,128,384]{4,3,2,1,0:T(8,128)(2,1)S(1)} %get-tuple-element.58), channel_id=1, source_target_pairs={{2,4},{4,6},{6,8},{8,10},{10,12},{12,14},{14,16},{16,18},{18,20},{... | collective-permute-start | bytes 2359304 | tf_op jit(solution)/shard_map/ppermute | solution.py:332
  48.8 0.7 pass_kernel.3
  49.4 7.6 %collective-permute-start.6 = (bf16[2,2,2,128,384]{4,3,2,1,0:T(8,128)(2,1)S(1)}, bf16[2,2,2,128,384]{4,3,2,1,0:T(8,128)(2,1)S(1)}, u32[]{:S(2)}, u32[]{:S(2)}) collective-permute-start(bf16[2,2,2,128,384]{4,3,2,1,0:T(8,128)(2,1)S(1)} %get-tuple-element.65), channel_id=1, source_target_pairs={{2,0},{4,2},{6,4},{8,6},{10,8},{12,10},{14,12},{16,14},{18,16},{20... | collective-permute-start | bytes 2359304 | tf_op jit(solution)/shard_map/ppermute | solution.py:332
  57.0 6.1 %collective-permute-done.7.up_two = bf16[2,2,2,128,384]{4,3,2,1,0:T(8,128)(2,1)} collective-permute-done((bf16[2,2,2,128,384]{4,3,2,1,0:T(8,128)(2,1)}, bf16[2,2,2,128,384]{4,3,2,1,0:T(8,128)(2,1)}, u32[]{:S(2)}, u32[]{:S(2)}) %collective-permute-start.7) | collective-permute-done | bytes 786464 | tf_op jit(solution)/shard_map/ppermute | solution.py:324
  63.1 1.9 %collective-permute-start.8 = (bf16[2,2,2,128,384]{4,3,2,1,0:T(8,128)(2,1)S(1)}, bf16[2,2,2,128,384]{4,3,2,1,0:T(8,128)(2,1)S(1)}, u32[]{:S(2)}, u32[]{:S(2)}) collective-permute-start(bf16[2,2,2,128,384]{4,3,2,1,0:T(8,128)(2,1)S(1)} %get-tuple-element.77), channel_id=1, source_target_pairs={{0,250},{6,0},{8,2},{10,4},{12,6},{14,8},{16,10},{18,12},{20,14},{... | collective-permute-start | bytes 2359304 | tf_op jit(solution)/shard_map/ppermute | solution.py:332
  65.0 0.0 collective-permute-done.3.down_two
  65.0 4.6 %collective-permute-start.4 = (bf16[2,2,2,128,384]{4,3,2,1,0:T(8,128)(2,1)S(1)}, bf16[2,2,2,128,384]{4,3,2,1,0:T(8,128)(2,1)S(1)}, u32[]{:S(2)}, u32[]{:S(2)}) collective-permute-start(bf16[2,2,2,128,384]{4,3,2,1,0:T(8,128)(2,1)S(1)} %get-tuple-element.64), channel_id=1, source_target_pairs={{0,6},{2,8},{4,10},{6,12},{8,14},{10,16},{12,18},{14,20},{16,22},{... | collective-permute-start | bytes 2359304 | tf_op jit(solution)/shard_map/ppermute | solution.py:332
  69.6 7.7 %own_kernel.1 = (f32[4,2,128,384]{3,2,1,0:T(8,128)S(1)}, f32[4,2,128,384]{3,2,1,0:T(8,128)S(1)}, f32[4,2,128,384]{3,2,1,0:T(8,128)S(1)}, f32[4,2,128,384]{3,2,1,0:T(8,128)S(1)}) custom-call(s32[5,5]{1,0:T(8,128)S(1)} %get-tuple-element.47.count_ref, s32[5,32]{1,0:T(8,128)S(1)} %get-tuple-element.55.item_ref, f32[4,8]{1,0:T(4,128)S(1)} %copy-done.3, ...), custom_call_target="tpu_custom_call" | custom-call | bytes 27000000 | tf_op jit(solution)/shard_map/own_kernel/pallas_call | solution.py:422
  77.3 2.8 %near_kernel.1 = (f32[4,2,128,384]{3,2,1,0:T(8,128)S(1)}, f32[4,2,128,384]{3,2,1,0:T(8,128)S(1)}, f32[4,2,128,384]{3,2,1,0:T(8,128)S(1)}, f32[4,2,128,384]{3,2,1,0:T(8,128)S(1)}) custom-call(s32[5,5]{1,0:T(8,128)S(1)} %get-tuple-element.47.count_ref, ...), custom_call_target="tpu_custom_call", output_to_operand_aliasing={{0}: (9, {}), {1}: (10, {}), {2}: (11, {}), {3}: (12, {})} | custom-call | bytes 12000000 | tf_op jit(solution)/shard_map/near_kernel/pallas_call | solution.py:432
  80.2 10.4 %collective-permute-done.6.down_one = bf16[2,2,2,128,384]{4,3,2,1,0:T(8,128)(2,1)S(1)} collective-permute-done((bf16[2,2,2,128,384]{4,3,2,1,0:T(8,128)(2,1)S(1)}, bf16[2,2,2,128,384]{4,3,2,1,0:T(8,128)(2,1)S(1)}, u32[]{:S(2)}, u32[]{:S(2)}) %collective-permute-start.6) | collective-permute-done | bytes 786464 | tf_op jit(solution)/shard_map/ppermute | solution.py:332
  90.5 1.7 %far_kernel.1 = (f32[4,2,128,384]{3,2,1,0:T(8,128)S(1)}, f32[4,2,128,384]{3,2,1,0:T(8,128)S(1)}, f32[4,2,128,384]{3,2,1,0:T(8,128)S(1)}, f32[4,2,128,384]{3,2,1,0:T(8,128)S(1)}) custom-call(s32[5,5]{1,0:T(8,128)S(1)} %get-tuple-element.47.count_ref, ...), custom_call_target="tpu_custom_call", output_to_operand_aliasing={{0}: (9, {}), {1}: (10, {}), {2}: (11, {}), {3}: (12, {})} | custom-call | bytes 6000000 | tf_op jit(solution)/shard_map/far_kernel/pallas_call | solution.py:445
  92.2 5.2 %collective-permute-done.8.refs_0_ = bf16[2,2,2,128,384]{4,3,2,1,0:T(8,128)(2,1)S(1)} collective-permute-done((bf16[2,2,2,128,384]{4,3,2,1,0:T(8,128)(2,1)S(1)}, bf16[2,2,2,128,384]{4,3,2,1,0:T(8,128)(2,1)S(1)}, u32[]{:S(2)}, u32[]{:S(2)}) %collective-permute-start.8) | collective-permute-done | bytes 786464 | tf_op jit(solution)/shard_map/ppermute | solution.py:332
  97.4 2.1 %last_kernel.2 = (bf16[4,2,4,128,384]{4,3,2,1,0:T(8,128)(2,1)}, f32[4,2,128,384]{3,2,1,0:T(8,128)S(1)}, f32[4,2,128,384]{3,2,1,0:T(8,128)S(1)}) custom-call(s32[5,5]{1,0:T(8,128)S(1)} %get-tuple-element.47.count_ref, s32[5,32]{1,0:T(8,128)S(1)} %get-tuple-element.55.item_ref, f32[4,8]{1,0:T(4,128)S(1)} %copy-done.3, ...), custom_call_target="tpu_custom_call", output_to_operand_aliasing={{1}: (6, {}), {2}: (7, {})} | custom-call | bytes 6000000 | tf_op jit(solution)/shard_map/last_kernel/pallas_call | solution.py:460
  99.6 2.1 %last_kernel.3 = (bf16[4,2,4,128,384]{4,3,2,1,0:T(8,128)(2,1)}, f32[4,2,128,384]{3,2,1,0:T(8,128)S(1)}, f32[4,2,128,384]{3,2,1,0:T(8,128)S(1)}) custom-call(s32[5,5]{1,0:T(8,128)S(1)} %get-tuple-element.47.count_ref, s32[5,32]{1,0:T(8,128)S(1)} %get-tuple-element.55.item_ref, ...), custom_call_target="tpu_custom_call", output_to_operand_aliasing={{1}: (6, {}), {2}: (7, {}), {0}: (8, {})} | custom-call | bytes 6000000 | tf_op jit(solution)/shard_map/last_kernel/pallas_call | solution.py:460
  (14 shorter events, 0.0 us)
Async XLA Ops:
  3.4 42.7 %collective-permute-start.1 = (bf16[4,2,2,128,384]{4,3,2,1,0:T(8,128)(2,1)}, bf16[4,2,2,128,384]{4,3,2,1,0:T(8,128)(2,1)S(1)}, u32[]{:S(2)}, u32[]{:S(2)}) collective-permute-start(bf16[4,2,2,128,384]{4,3,2,1,0:T(8,128)(2,1)} %get-tuple-element.42), channel_id=1, source_target_pairs={{0,2},{2,4},{4,6},{6,8},{8,10},{10,12},{12,14},{14,16},{16,18},{18... | collective-permute-start | bytes 4718600 | tf_op jit(solution)/shard_map/ppermute | solution.py:324
  4.8 43.9 %collective-permute-start.2 = (bf16[4,2,2,128,384]{4,3,2,1,0:T(8,128)(2,1)}, bf16[4,2,2,128,384]{4,3,2,1,0:T(8,128)(2,1)S(1)}, u32[]{:S(2)}, u32[]{:S(2)}) collective-permute-start(bf16[4,2,2,128,384]{4,3,2,1,0:T(8,128)(2,1)} %get-tuple-element.60), channel_id=1, source_target_pairs={{0,254},{2,0},{4,2},{6,4},{8,6},{10,8},{12,10},{14,12},{16,14},{18... | collective-permute-start | bytes 4718600 | tf_op jit(solution)/shard_map/ppermute | solution.py:324
  11.9 11.4 %copy-start.2 = (s32[512,8]{0,1:T(8,128)S(1)}, s32[512,8]{0,1:T(8,128)}, u32[]{:S(2)}) copy-start(s32[512,8]{0,1:T(8,128)} %param.9) | copy-start | bytes 49156
  16.0 47.1 %collective-permute-start.7 = (bf16[2,2,2,128,384]{4,3,2,1,0:T(8,128)(2,1)}, bf16[2,2,2,128,384]{4,3,2,1,0:T(8,128)(2,1)}, u32[]{:S(2)}, u32[]{:S(2)}) collective-permute-start(bf16[2,2,2,128,384]{4,3,2,1,0:T(8,128)(2,1)} %get-tuple-element.44), channel_id=1, source_target_pairs={{0,2},{2,4},{4,6},{6,8},{8,10},{10,12},{12,14},{14,16},{16,18},{18... | collective-permute-start | bytes 2359304 | tf_op jit(solution)/shard_map/ppermute | solution.py:324
  16.1 48.9 %collective-permute-start.3 = (bf16[2,2,2,128,384]{4,3,2,1,0:T(8,128)(2,1)}, bf16[2,2,2,128,384]{4,3,2,1,0:T(8,128)(2,1)}, u32[]{:S(2)}, u32[]{:S(2)}) collective-permute-start(bf16[2,2,2,128,384]{4,3,2,1,0:T(8,128)(2,1)} %get-tuple-element.63), channel_id=1, source_target_pairs={{0,254},{2,0},{4,2},{6,4},{8,6},{10,8},{12,10},{14,12},{16,14},{18... | collective-permute-start | bytes 2359304 | tf_op jit(solution)/shard_map/ppermute | solution.py:324
  21.7 8.9 %collective-permute-start = (bf16[4,2,4,16,384]{4,3,2,1,0:T(8,128)(2,1)}, bf16[4,2,4,16,384]{4,3,2,1,0:T(8,128)(2,1)S(1)}, u32[]{:S(2)}, u32[]{:S(2)}) collective-permute-start(bf16[4,2,4,16,384]{4,3,2,1,0:T(8,128)(2,1)} %get-tuple-element.54), channel_id=1, source_target_pairs={{0,1},{1,0},{2,3},{3,2},{4,5},{5,4},{6,7},{7,6},{8,9},{9,8},{10,11... | collective-permute-start | bytes 1179656 | tf_op jit(solution)/shard_map/ppermute | solution.py:359
  23.3 0.7 copy-start.4
  23.9 0.7 copy-start.6
  24.6 0.7 copy-start.7
  30.7 2.3 %copy-start = (bf16[4,2,6,128,384]{4,3,2,1,0:T(8,128)(2,1)S(1)}, bf16[4,2,6,128,384]{4,3,2,1,0:T(8,128)(2,1)}, u32[]{:S(2)}) copy-start(bf16[4,2,6,128,384]{4,3,2,1,0:T(8,128)(2,1)} %wave_ref.4) | copy-start | bytes 14155780
  33.0 0.7 copy-start.5
  33.7 35.9 %copy-start.1 = (bf16[4,2,6,128,384]{4,3,2,1,0:T(8,128)(2,1)S(1)}, bf16[4,2,6,128,384]{4,3,2,1,0:T(8,128)(2,1)}, u32[]{:S(2)}) copy-start(bf16[4,2,6,128,384]{4,3,2,1,0:T(8,128)(2,1)} %wave_ref.4) | copy-start | bytes 14155780
  40.8 28.8 %copy-start.3 = (f32[4,8]{1,0:T(4,128)S(1)}, f32[4,8]{1,0:T(4,128)}, u32[]{:S(2)}) copy-start(f32[4,8]{1,0:T(4,128)} %weight_ref.4) | copy-start | bytes 388
  46.8 33.3 %collective-permute-start.5 = (bf16[2,2,2,128,384]{4,3,2,1,0:T(8,128)(2,1)S(1)}, bf16[2,2,2,128,384]{4,3,2,1,0:T(8,128)(2,1)S(1)}, u32[]{:S(2)}, u32[]{:S(2)}) collective-permute-start(bf16[2,2,2,128,384]{4,3,2,1,0:T(8,128)(2,1)S(1)} %get-tuple-element.58), channel_id=1, source_target_pairs={{2,4},{4,6},{6,8},{8,10},{10,12},{12,14},{14,16},{16,18},{18,20},{... | collective-permute-start | bytes 2359304 | tf_op jit(solution)/shard_map/ppermute | solution.py:332
  49.4 41.1 %collective-permute-start.6 = (bf16[2,2,2,128,384]{4,3,2,1,0:T(8,128)(2,1)S(1)}, bf16[2,2,2,128,384]{4,3,2,1,0:T(8,128)(2,1)S(1)}, u32[]{:S(2)}, u32[]{:S(2)}) collective-permute-start(bf16[2,2,2,128,384]{4,3,2,1,0:T(8,128)(2,1)S(1)} %get-tuple-element.65), channel_id=1, source_target_pairs={{2,0},{4,2},{6,4},{8,6},{10,8},{12,10},{14,12},{16,14},{18,16},{20... | collective-permute-start | bytes 2359304 | tf_op jit(solution)/shard_map/ppermute | solution.py:332
  63.1 34.3 %collective-permute-start.8 = (bf16[2,2,2,128,384]{4,3,2,1,0:T(8,128)(2,1)S(1)}, bf16[2,2,2,128,384]{4,3,2,1,0:T(8,128)(2,1)S(1)}, u32[]{:S(2)}, u32[]{:S(2)}) collective-permute-start(bf16[2,2,2,128,384]{4,3,2,1,0:T(8,128)(2,1)S(1)} %get-tuple-element.77), channel_id=1, source_target_pairs={{0,250},{6,0},{8,2},{10,4},{12,6},{14,8},{16,10},{18,12},{20,14},{... | collective-permute-start | bytes 2359304 | tf_op jit(solution)/shard_map/ppermute | solution.py:332
  65.0 34.5 %collective-permute-start.4 = (bf16[2,2,2,128,384]{4,3,2,1,0:T(8,128)(2,1)S(1)}, bf16[2,2,2,128,384]{4,3,2,1,0:T(8,128)(2,1)S(1)}, u32[]{:S(2)}, u32[]{:S(2)}) collective-permute-start(bf16[2,2,2,128,384]{4,3,2,1,0:T(8,128)(2,1)S(1)} %get-tuple-element.64), channel_id=1, source_target_pairs={{0,6},{2,8},{4,10},{6,12},{8,14},{10,16},{12,18},{14,20},{16,22},{... | collective-permute-start | bytes 2359304 | tf_op jit(solution)/shard_map/ppermute | solution.py:332
